TPU v7x, 32 devices: a whole 2x2x4 slice. The times are simulated.
32 devices in a mesh: dp: 8 (over z, x), frame: 4 (over y, core).
Axes of the slice: x: 2, y: 2, z: 4, core: 2. Of those that a mesh axis runs over, the one named last changes fastest.
Arguments:
- enc_rows: bfloat16 [4096, 512], P(('dp', 'frame')), may hold values from -6 to 6
- dest: int32 [8, 4, 128], P(None, 'frame'), may hold values from 0 to 1023, as said below
- pred_rows: bfloat16 [1024, 512], P(('dp', 'frame')), may hold values from -6 to 6
- label_ids: int32 [8, 128], P('dp'), may hold values from 1 to 499
- block_off: int32 [64], P(('dp', 'frame')), may hold values from 0 to 64
- band_start: int32 [4096], P(('dp', 'frame')), may hold values from 0 to 61
- w_enc: bfloat16 [512, 512], replicated, may hold values from -0.25 to 0.25
- w_dec: bfloat16 [512, 512], replicated, may hold values from -0.25 to 0.25
- w_out: bfloat16 [512, 500], replicated
- bias_out: float32 [500], replicated, may hold values from -4 to 4
- grad_blank: float32 [4096, 3], P(('dp', 'frame')), may hold values from -6 to 6
- grad_label: float32 [4096, 3], P(('dp', 'frame')), may hold values from -6 to 6
Outputs:
- logprobs: float32 [4096, 6], P(('dp', 'frame'))
- grad_enc: bfloat16 [4096, 512], P(('dp', 'frame'))
- grad_pred: float32 [1024, 512], P(('dp', 'frame'))
- grad_w_out: float32 [512, 500], P(('dp', 'frame'))
Inputs may be any that keep to these rules, and one draw needn't show every extreme that they name: For each frame shard f, dest[:, f, :] holds every value 0 to 1023 once; at most 32 rows of one loader shard go to one owner, exactly 32 for some pairs; the rows one loader shard sends one owner take consecutive owner rows, in increasing order of the sending shard.
All inputs are finite; a program needn't handle non-finite values.
Results may differ from a plain program's by a relative error of at most 0.01.
Values may be sent and summed in bfloat16 or wider, within the bound.
A program may use at most 64 MiB of HBM per device.

v0:
```python
import jax
import jax.numpy as jnp
from jax import lax
from jax.sharding import PartitionSpec as P

BLOCK = 64


def shards(
    enc_rows,
    dest,
    pred_rows,
    label_ids,
    block_off,
    band_start,
    w_enc,
    w_dec,
    w_out,
    bias_out,
    grad_blank,
    grad_label,
):
    owners = lax.axis_size("dp")
    shard_count = lax.axis_size("frame")
    my_index = lax.axis_index("dp")
    row_count, feat_width = enc_rows.shape
    slot_cap = 2 * row_count // owners
    dest_table = dest[:, 0, :]
    owner_of = dest_table // row_count
    source_ids = jnp.arange(owners, dtype=jnp.int32)
    pair_counts = jax.ops.segment_sum(
        jnp.ones((owners * row_count,), jnp.int32),
        (source_ids[:, None] * owners + owner_of).reshape(-1),
        num_segments=owners * owners,
    ).reshape(owners, owners)
    pair_offsets = jnp.cumsum(pair_counts, axis=0) - pair_counts
    my_dest = lax.dynamic_index_in_dim(dest_table, my_index, 0, keepdims=False)
    my_owner = my_dest // row_count
    my_offsets = lax.dynamic_index_in_dim(pair_offsets, my_index, 0, keepdims=False)
    owner_match = my_owner[:, None] == source_ids[None, :]
    my_rank = my_dest % row_count - jnp.sum(jnp.where(owner_match, my_offsets[None, :], 0), axis=1)
    my_slot = my_owner * slot_cap + my_rank
    outbound = jnp.zeros((owners * slot_cap, feat_width), enc_rows.dtype).at[my_slot].set(enc_rows)
    arrived = lax.all_to_all(
        outbound.reshape(owners, slot_cap, feat_width),
        "dp",
        split_axis=0,
        concat_axis=0,
        tiled=True,
    )
    in_count = lax.dynamic_index_in_dim(pair_counts, my_index, 1, keepdims=False)
    in_offset = lax.dynamic_index_in_dim(pair_offsets, my_index, 1, keepdims=False)
    slot_iota = jnp.arange(slot_cap, dtype=jnp.int32)
    live_slot = slot_iota[None, :] < in_count[:, None]
    owner_rows = in_offset[:, None] + slot_iota[None, :]
    put_index = jnp.where(live_slot, owner_rows, row_count).reshape(-1)
    enc_owned = (
        jnp.zeros((row_count, feat_width), enc_rows.dtype)
        .at[put_index]
        .set(arrived.reshape(-1, feat_width), mode="drop")
    )
    enc_joint = jnp.dot(enc_owned, w_enc, preferred_element_type=jnp.float32)
    w_dec_float = w_dec.astype(jnp.float32)
    dec_joint = jnp.dot(
        lax.all_gather(pred_rows, "frame", axis=0, tiled=True),
        w_dec,
        preferred_element_type=jnp.float32,
    ).astype(jnp.bfloat16)
    block_rows = BLOCK
    kept = grad_blank.shape[1]
    joint_width = enc_joint.shape[1]
    band_base = (block_off[:, None] + jnp.zeros((1, block_rows), jnp.int32)).reshape(
        -1
    ) + band_start
    label_pos = band_base[:, None] + jnp.arange(kept, dtype=jnp.int32)[None, :]
    flat_pos = label_pos.reshape(-1)
    label_row_ids = label_ids[0]
    emitted = label_row_ids[flat_pos]
    vocab_ids = jnp.arange(w_out.shape[1], dtype=jnp.int32)
    summed = enc_joint[:, None, :] + dec_joint[label_pos].astype(jnp.float32)
    hidden_all = jnp.tanh(summed).astype(jnp.bfloat16).reshape(row_count * kept, joint_width)
    logits = jnp.dot(hidden_all, w_out, preferred_element_type=jnp.float32) + bias_out
    logp = jax.nn.log_softmax(logits, axis=-1)
    blank_part = logp[:, 0].reshape(row_count, kept)
    label_part = jnp.take_along_axis(logp, emitted[:, None], axis=1)[:, 0].reshape(row_count, kept)
    logprobs = jnp.concatenate([blank_part, label_part], axis=1)
    cot_blank = grad_blank.reshape(-1)[:, None]
    cot_label = grad_label.reshape(-1)[:, None]
    dlogit_all = (
        cot_blank * (vocab_ids[None, :] == 0)
        + cot_label * (vocab_ids[None, :] == emitted[:, None])
        - jnp.exp(logp) * (cot_blank + cot_label)
    ).astype(jnp.bfloat16)
    back_hidden = lax.dot_general(
        dlogit_all, w_out, (((1,), (1,)), ((), ())), preferred_element_type=jnp.float32
    )
    hidden_f = hidden_all.astype(jnp.float32)
    dz_all = back_hidden * (1.0 - hidden_f * hidden_f)
    enc_grad_j = jnp.sum(dz_all.reshape(row_count, kept, joint_width), axis=1)
    dec_grad_j = jnp.zeros((dec_joint.shape[0], joint_width), jnp.float32).at[flat_pos].add(dz_all)
    per_device = joint_width // (owners * shard_count)
    wanted = jnp.arange(lax.axis_size("frame") * (joint_width // shard_count), dtype=jnp.int32)
    frame_part = wanted // (owners * per_device)
    remainder = wanted % (owners * per_device)
    owner_part = remainder // per_device
    inner_part = remainder % per_device
    initial = (owner_part * shard_count + frame_part) * per_device + inner_part
    chosen = jnp.take(hidden_all, initial, axis=1)
    frame_sums = lax.psum_scatter(
        lax.dot_general(
            chosen, dlogit_all, (((0,), (0,)), ((), ())), preferred_element_type=jnp.float32
        ).astype(jnp.bfloat16),
        "frame",
        scatter_dimension=0,
        tiled=True,
    ).astype(jnp.float32)
    grad_w_out = lax.psum_scatter(frame_sums, "dp", scatter_dimension=0, tiled=True)
    grad_pred = lax.psum_scatter(
        jnp.dot(dec_grad_j, w_dec_float.T, precision=lax.Precision.HIGHEST).astype(jnp.bfloat16),
        "frame",
        scatter_dimension=0,
        tiled=True,
    ).astype(jnp.float32)
    owned_grad = lax.dot_general(
        enc_grad_j.astype(jnp.bfloat16),
        w_enc,
        (((1,), (1,)), ((), ())),
        preferred_element_type=jnp.float32,
    ).astype(jnp.bfloat16)
    get_index = jnp.where(live_slot, owner_rows, 0).reshape(-1)
    outgoing = jnp.where(
        live_slot.reshape(-1)[:, None], owned_grad[get_index], jnp.zeros((), owned_grad.dtype)
    )
    returned = lax.all_to_all(
        outgoing.reshape(owners, slot_cap, feat_width),
        "dp",
        split_axis=0,
        concat_axis=0,
        tiled=True,
    )
    grad_enc = returned.reshape(owners * slot_cap, feat_width)[my_slot]
    return (logprobs, grad_enc, grad_pred, grad_w_out)


def solution(mesh):
    return jax.shard_map(
        shards,
        mesh=mesh,
        in_specs=(
            P(("dp", "frame"), None),
            P(None, "frame", None),
            P(("dp", "frame"), None),
            P("dp", None),
            P(("dp", "frame")),
            P(("dp", "frame")),
            P(),
            P(),
            P(),
            P(),
            P(("dp", "frame"), None),
            P(("dp", "frame"), None),
        ),
        out_specs=(
            P(("dp", "frame"), None),
            P(("dp", "frame"), None),
            P(("dp", "frame"), None),
            P(("dp", "frame"), None),
        ),
        check_vma=False,
    )
```

profile of v0, /device:TPU:0, one launch (start us, length us, event | category | flops | bytes accessed | tf_op | source)
XLA Modules:
  0.0 168.6 jit_solution(36242550981237122)
XLA Ops:
  7.2 0.7 copy-done.5
  8.1 7.6 %scatter_custom_fusion = s32[64]{0:T(128)S(1)} fusion(s32[1024]{0:T(1024)S(1)} %bitcast.76, s32[1024]{0:T(1024)S(1)} %broadcast.650, s32[]{:T(128)} %constant.151.clone.1), kind=kCustom, calls=%fused_computation.129 | custom fusion | flops 1024 | bytes 260 | tf_op jit(solution)/shard_map/scatter-add | solution.py:31
  15.9 2.1 %scatter_custom_fusion.1 = bf16[256,512]{1,0:T(8,128)(2,1)} fusion(s32[128]{0:T(128)S(1)} %fusion.38, bf16[128,512]{1,0:T(8,128)(2,1)} %param.12, bf16[]{:T(256)} %constant.150.clone.1), kind=kCustom, calls=%fused_computation.30 | custom fusion | bytes 262656 | tf_op jit(solution)/shard_map/scatter | solution.py:43
  18.0 7.3 %all-to-all-start = ((bf16[8,32,512]{2,1,0:T(8,128)(2,1)}), bf16[8,32,512]{2,1,0:T(8,128)(2,1)S(1)}, u32[]{:S(2)}, u32[]{:S(2)}) async-start(bf16[8,32,512]{2,1,0:T(8,128)(2,1)} %bitcast.9), calls=%async_computation | async-start | bytes 524288 | tf_op jit(solution)/shard_map/all_to_all | solution.py:44
  25.4 0.2 dynamic-slice_reduce_fusion
  25.6 0.4 copy-done.9
  26.2 0.6 copy-done.10
  26.9 0.2 add.391
  27.2 0.6 copy-done.1
  27.8 2.7 %gather_fusion.1 = s32[384]{0:T(512)S(1)} fusion(s32[128]{0:T(128)S(1)} %bitcast.70, s32[1024]{0:T(1024)S(1)} %pad_clamp_fusion.3), kind=kCustom, calls=%fused_computation.1 | custom fusion | bytes 4608 | tf_op jit(solution)/shard_map/gather | solution.py:78
  30.8 0.5 copy-done.4
  31.3 5.4 %all_gather.3 = bf16[128,512]{1,0:T(8,128)(2,1)S(1)} all-gather(bf16[32,512]{1,0:T(8,128)(2,1)S(1)} %copy-done.4), channel_id=1, replica_groups=mesh['dp'=8,'frame'=4] {'frame'}, dimensions={0}, use_global_device_ids=true | all-gather | bytes 163840 | tf_op jit(solution)/shard_map/all_gather | solution.py:65
  36.8 0.2 convolution_convert_fusion.3
  37.2 0.6 copy-done.7
  38.1 0.5 copy-done.8
  38.7 0.2 mul.97
  38.9 2.1 %gather_fusion = bf16[384,512]{1,0:T(8,128)(2,1)S(1)} fusion(bf16[128,512]{1,0:T(8,128)(2,1)S(1)} %convolution_convert_fusion.3, s32[1024]{0:T(1024)S(1)} %pad_clamp_fusion.4), kind=kCustom, calls=%fused_computation | custom fusion | bytes 787968 | tf_op jit(solution)/shard_map/gather | solution.py:80
  41.0 0.4 reshape.712
  41.4 1.5 scatter_custom_fusion.2
  42.9 0.2 fusion.43
  43.2 0.4 tanh_convert_fusion
  43.6 0.3 convert_element_type.52
  44.0 0.2 copy.34
  44.2 0.8 copy-done.3
  45.0 0.5 fusion.42
  45.7 2.6 %gather_fusion.4 = bf16[512,384]{1,0:T(8,128)(2,1)} fusion(bf16[384,512]{0,1:T(8,128)(2,1)S(1)} %copy.34, s32[1024]{0:T(1024)S(1)} %pad_clamp_fusion), kind=kCustom, calls=%fused_computation.4 | custom fusion | bytes 788480 | tf_op jit(solution)/shard_map/jit(_take)/gather | solution.py:108
  48.3 1.6 convolution_convert_fusion
  49.9 1.0 copy.36
  50.9 0.2 reduce-scatter.8.cloned.1.call-start
  51.3 1.5 convolution_multiply_fusion
  52.8 1.5 reshape.628
  54.2 3.5 %scatter_custom_fusion.3 = f32[128,512]{1,0:T(8,128)S(1)} fusion(s32[384]{0:T(512)S(1)} %fusion.30, f32[384,512]{1,0:T(8,128)} %convolution_multiply_fusion, f32[]{:T(128)} %constant.163.clone.1), kind=kCustom, calls=%fused_computation.27 | custom fusion | flops 196608 | bytes 262656 | tf_op jit(solution)/shard_map/scatter-add | solution.py:100
  57.7 0.7 reduce_sum.33
  58.4 1.3 convolution_convert_fusion.1
  59.7 0.3 convolution_convert_fusion.2
  60.0 1.2 gather_fusion.2
  61.2 0.8 broadcast_select_fusion
  62.0 5.9 %all-to-all-start.1 = ((bf16[8,32,512]{2,1,0:T(8,128)(2,1)}), bf16[8,32,512]{2,1,0:T(8,128)(2,1)S(1)}, u32[]{:S(2)}, u32[]{:S(2)}) async-start(bf16[8,32,512]{2,1,0:T(8,128)(2,1)} %broadcast_select_fusion), calls=%async_computation.1 | async-start | bytes 524288 | tf_op jit(solution)/shard_map/all_to_all | solution.py:134
  68.0 6.2 %reduce-scatter.10.cloned.1.call-done = bf16[128,500]{1,0:T(8,128)(2,1)} async-done(((bf16[512,500]{1,0:T(8,128)(2,1)}), bf16[128,500]{1,0:T(8,128)(2,1)}) %reduce-scatter.10.cloned.1.call-update) | async-done | bytes 128016
  74.2 1.1 copy.37
  75.3 0.9 copy.38
  76.3 3.5 %gather_fusion.5 = f32[384]{0:T(512)S(1)} fusion(f32[384,500]{0,1:T(8,128)S(1)} %subtract_subtract_fusion, s32[384]{0:T(512)S(1)} %fusion.34), kind=kCustom, calls=%fused_computation.5 | custom fusion | bytes 6144 | tf_op jit(solution)/shard_map/jit(take_along_axis)/gather | solution.py:85
  80.1 0.2 gather.33
  80.4 0.6 pad_maximum_fusion
  81.1 15.9 %reduce-scatter.8.cloned.1.call-done = bf16[32,512]{1,0:T(8,128)(2,1)} async-done(((bf16[128,512]{1,0:T(8,128)(2,1)}), bf16[32,512]{1,0:T(8,128)(2,1)}) %reduce-scatter.8.cloned.1.call-update) | async-done | bytes 32784 | tf_op jit(solution)/shard_map/reduce_scatter | solution.py:118
  97.0 1.4 convert_element_type.59
  98.4 1.5 gather_fusion.3
  99.9 62.2 %reduce-scatter.12.cloned.1.call-done = f32[16,500]{1,0:T(8,128)} async-done(((f32[128,500]{1,0:T(8,128)}), f32[16,500]{1,0:T(8,128)}) %reduce-scatter.12.cloned.1.call-update) | async-done | bytes 32016
  (70 shorter events, 2.7 us)
Async XLA Ops:
  7.2 29.6 %copy-start = (bf16[512,512]{1,0:T(8,128)(2,1)S(1)}, bf16[512,512]{1,0:T(8,128)(2,1)}, u32[]{:S(2)}) copy-start(bf16[512,512]{1,0:T(8,128)(2,1)} %param.19) | copy-start | bytes 1572868
  7.2 0.7 copy-start.5
  18.0 23.4 %all-to-all-start = ((bf16[8,32,512]{2,1,0:T(8,128)(2,1)}), bf16[8,32,512]{2,1,0:T(8,128)(2,1)S(1)}, u32[]{:S(2)}, u32[]{:S(2)}) async-start(bf16[8,32,512]{2,1,0:T(8,128)(2,1)} %bitcast.9), calls=%async_computation | async-start | bytes 524288 | tf_op jit(solution)/shard_map/all_to_all | solution.py:44
  25.3 48.9 %reduce-scatter.10.cloned.1.call-start = ((), (), s32[]{:S(2)}) async-start(), calls=%async_computation.6 | async-start | bytes 655360
  25.3 0.7 copy-start.9
  26.1 0.7 copy-start.10
  27.2 0.7 copy-start.1
  30.5 0.8 copy-start.4
  37.1 0.7 copy-start.7
  37.9 0.7 copy-start.8
  41.0 2.0 %copy-start.2 = (bf16[512,512]{1,0:T(8,128)(2,1)S(1)}, bf16[512,512]{1,0:T(8,128)(2,1)}, u32[]{:S(2)}) copy-start(bf16[512,512]{1,0:T(8,128)(2,1)} %param.18) | copy-start | bytes 1572868
  43.9 1.0 copy-start.3
  43.9 1.0 copy-start.6
  50.9 46.0 %reduce-scatter.8.cloned.1.call-start = ((), (), s32[]{:S(2)}) async-start(), calls=%async_computation.5 | async-start | bytes 163840 | tf_op jit(solution)/shard_map/reduce_scatter | solution.py:118
  62.0 36.4 %all-to-all-start.1 = ((bf16[8,32,512]{2,1,0:T(8,128)(2,1)}), bf16[8,32,512]{2,1,0:T(8,128)(2,1)S(1)}, u32[]{:S(2)}, u32[]{:S(2)}) async-start(bf16[8,32,512]{2,1,0:T(8,128)(2,1)} %broadcast_select_fusion), calls=%async_computation.1 | async-start | bytes 524288 | tf_op jit(solution)/shard_map/all_to_all | solution.py:134
  67.9 94.2 %reduce-scatter.12.cloned.1.call-start = ((), (), s32[]{:S(2)}) async-start(), calls=%async_computation.7 | async-start | bytes 294912
Sparse Core Ops, SparseCore 0:
  51.1 23.0 reduce-scatter.9
  77.3 19.6 reduce-scatter.7
  100.9 61.1 reduce-scatter.11
where the time goes:
time: 169 us
  waiting for transfers between devices  84.4 us (50%)
  local copies, waits for them, and re-layouts  29.7 us (18%)
  other arithmetic  15.9 us (9%)
  between operations  14.2 us (8%)
  starting transfers between devices  13.5 us (8%)
  matrix products  5.62 us (3%)
  blocking collectives  5.41 us (3%)
    unnamed x5, waiting for transfers between devices  68.5 us
    reduce_scatter x1, waiting for transfers between devices, shards(): lax.psum_scatter(jnp.dot(dec_grad_j, w_dec_float.T, precision=lax.Precisi...  15.9 us
    unnamed x28, local copies, waits for them, and re-layouts  7.98 us
    scatter-add x1, other arithmetic, shards(): jax.ops.segment_sum(jnp.ones((owners * row_count,), jnp.int32), (source_i...  7.61 us
    all_to_all x1, starting transfers between devices, shards(): lax.all_to_all(outbound.reshape(owners, slot_cap, feat_width), 'dp', spli...  7.25 us
    all_to_all x1, starting transfers between devices, shards(): lax.all_to_all(outgoing.reshape(owners, slot_cap, feat_width), 'dp', spli...  5.95 us
    all_gather x1, blocking collectives, shards(): lax.all_gather(pred_rows, 'frame', axis=0, tiled=True)  5.41 us
    gather x2, local copies, waits for them, and re-layouts, shards(): jnp.take_along_axis(logp, emitted[:, None], axis=1)[:, 0]  3.69 us
  transfers between devices with their start and end apart: 5, of which 3 were waited for; matrix products, arithmetic and copies ran while one was open for 16% of the time, Pallas kernels for 0%

commit v1 on v0

v1 whole, which is shorter than its diff:
```python
import functools

import jax
import jax.numpy as jnp
from jax import lax
from jax.experimental import pallas as pl
from jax.experimental.pallas import tpu as pltpu
from jax.sharding import PartitionSpec as P

BLOCK = 64
TILE_ROWS = 16
MASKED = -1e30
MESH = pl.DeviceIdType.MESH


def log2(size):
    assert size & (size - 1) == 0
    return size.bit_length() - 1


def joint_kernel(
    dims,
    enc_ref,
    dest_ref,
    pred_ref,
    label_ref,
    off_ref,
    band_ref,
    w_enc_ref,
    w_dec_ref,
    w_out_ref,
    bias_ref,
    blank_ref,
    cot_ref,
    logp_ref,
    grad_enc_ref,
    grad_pred_ref,
    grad_w_ref,
    outbound,
    arrived,
    outgoing,
    returned,
    pred_all,
    gw_send,
    gw_recv,
    gw2_send,
    gw2_recv,
    gp_send,
    gp_recv,
    dp_sem,
    frame_sem,
):
    owners, shards, cap, rows, kept, reduce_here = dims
    me = lax.axis_index("dp")
    part = lax.axis_index("frame")
    width = enc_ref.shape[1]
    joint = w_enc_ref.shape[1]
    vocab = w_out_ref.shape[0]
    lab_part = pred_ref.shape[0]
    labels = shards * lab_part
    slots = owners * cap
    f32, bf16 = jnp.float32, jnp.bfloat16

    def iota(shape, dim):
        return lax.broadcasted_iota(jnp.int32, shape, dim)

    def to_owner(step, src, dst, kind):
        peer = lax.rem(me + step, owners)
        return pltpu.make_async_remote_copy(
            src_ref=src(peer),
            dst_ref=dst(step),
            send_sem=dp_sem.at[kind, 0, step],
            recv_sem=dp_sem.at[kind, 1, step],
            device_id={"dp": peer},
            device_id_type=MESH,
        )

    def to_shard(step, src, dst, kind):
        peer = lax.rem(part + step, shards)
        return pltpu.make_async_remote_copy(
            src_ref=src(peer),
            dst_ref=dst(step),
            send_sem=frame_sem.at[kind, 0, step],
            recv_sem=frame_sem.at[kind, 1, step],
            device_id={"frame": peer},
            device_id_type=MESH,
        )

    def each(count, act):
        if count <= 8:
            for step in range(1, count):
                act(step)
        else:

            def body(step, carry):
                act(step)
                return carry

            lax.fori_loop(1, count, body, 0)

    barrier = pltpu.get_barrier_semaphore()

    def greet_owner(step):
        pl.semaphore_signal(
            barrier, inc=1, device_id={"dp": lax.rem(me + step, owners)}, device_id_type=MESH
        )

    def greet_shard(step):
        pl.semaphore_signal(
            barrier, inc=1, device_id={"frame": lax.rem(part + step, shards)}, device_id_type=MESH
        )

    each(owners, greet_owner)
    each(shards, greet_shard)

    shape = (slots, rows)
    slot_owner = lax.shift_right_logical(iota(shape, 0), log2(cap))
    slot_rank = iota(shape, 0) & (cap - 1)
    lane = iota(shape, 1)
    my_dest = dest_ref[pl.ds(me, 1), :]

    def count(source, sums):
        out_sum, in_sum = sums
        owner_of = lax.shift_right_logical(dest_ref[pl.ds(source, 1), :], log2(rows))
        before_me = (source < me).astype(f32)
        out_sum = out_sum + jnp.where(owner_of == slot_owner, before_me, 0.0)
        mine = jnp.where(owner_of == me, 1.0, 0.0)
        in_sum = in_sum + jnp.where(slot_owner > source, mine, 0.0)
        return out_sum, in_sum

    sums = (jnp.zeros(shape, f32), jnp.zeros(shape, f32))
    if owners <= 8:
        for source in range(owners):
            sums = count(source, sums)
    else:
        sums = lax.fori_loop(0, owners, count, sums)
    out_row = jnp.sum(sums[0], axis=1, keepdims=True).astype(jnp.int32) + slot_rank
    in_row = jnp.sum(sums[1], axis=1, keepdims=True).astype(jnp.int32) + slot_rank
    pick = (my_dest == slot_owner * rows + out_row) & (out_row < rows)
    pick = jnp.where(pick, 1.0, 0.0)
    place = jnp.where(lane == in_row, 1.0, 0.0)
    out_rows = jnp.dot(pick.astype(bf16), enc_ref[...], preferred_element_type=f32).astype(bf16)
    outbound[...] = out_rows.reshape(owners, cap, width)

    pl.semaphore_wait(barrier, owners - 1 + shards - 1)

    send_enc = functools.partial(
        to_owner, src=lambda peer: outbound.at[peer], dst=lambda step: arrived.at[me], kind=0
    )
    send_pred = functools.partial(
        to_shard, src=lambda peer: pred_ref, dst=lambda step: pred_all.at[part], kind=0
    )
    each(owners, lambda step: send_enc(step).start())
    each(shards, lambda step: send_pred(step).start())
    arrived[me] = outbound[me]
    pred_all[part] = pred_ref[...]

    half = iota((1, rows), 1) // BLOCK
    base_row = band_ref[...]
    for block in range(rows // BLOCK):
        base_row = base_row + jnp.where(half == block, off_ref[block], 0)
    cols = jnp.concatenate(
        [
            base_row.astype(f32),
            jnp.zeros((1, rows), f32),
            blank_ref[...],
            cot_ref[...],
        ],
        axis=0,
    ).T
    base_col = cols[:, 0:1].astype(jnp.int32)
    gather_hot = jnp.concatenate(
        [
            jnp.where(iota((rows, labels), 1) == base_col + k, 1.0, 0.0)
            for k in range(kept)
        ],
        axis=0,
    )
    scatter_hot = jnp.concatenate(
        [
            jnp.where(iota((labels, rows), 0) == base_row + k, 1.0, 0.0)
            for k in range(kept)
        ],
        axis=1,
    ).astype(bf16)
    emitted = jnp.sum(gather_hot * label_ref[...].astype(f32), axis=1, keepdims=True)
    emitted = emitted.astype(jnp.int32)
    place_t = place.T.astype(bf16)
    pick_t = pick.T.astype(bf16)
    place = place.astype(bf16)

    each(shards, lambda step: send_pred(step).wait())
    dec_joint = jnp.dot(
        pred_all[...].reshape(labels, width), w_dec_ref[...], preferred_element_type=f32
    ).astype(bf16)
    dec_rows = jnp.dot(gather_hot.astype(bf16), dec_joint, preferred_element_type=f32)

    each(owners, lambda step: send_enc(step).wait())
    enc_owned = jnp.dot(
        place_t, arrived[...].reshape(slots, width), preferred_element_type=f32
    ).astype(bf16)
    enc_joint = jnp.dot(enc_owned, w_enc_ref[...], preferred_element_type=f32)
    hidden = jnp.tanh(jnp.concatenate([enc_joint] * kept, axis=0) + dec_rows).astype(bf16)
    logits = (
        lax.dot_general(
            hidden, w_out_ref[...], (((1,), (1,)), ((), ())), preferred_element_type=f32
        )
        + bias_ref[...]
    )
    top = jnp.max(logits, axis=1, keepdims=True)
    shifted = logits - top
    powers = jnp.exp(shifted)
    total = jnp.sum(powers, axis=1, keepdims=True)
    log_total = jnp.log(total)
    word = iota((rows * kept, vocab), 1)
    is_label = word == emitted
    blank_logp = shifted[:, 0:1] - log_total
    label_logp = jnp.sum(jnp.where(is_label, shifted, 0.0), axis=1, keepdims=True) - log_total
    cot_blank = jnp.concatenate([cols[:, 2 + k : 3 + k] for k in range(kept)], axis=0)
    cot_label = jnp.concatenate([cols[:, 2 + kept + k : 3 + kept + k] for k in range(kept)], axis=0)
    scale = (cot_blank + cot_label) / total
    dlogit = (
        jnp.where(word == 0, cot_blank, 0.0) + jnp.where(is_label, cot_label, 0.0) - powers * scale
    ).astype(bf16)

    grad_w = lax.dot_general(
        hidden, dlogit, (((0,), (0,)), ((), ())), preferred_element_type=f32
    ).astype(bf16)
    if reduce_here:
        gw_send[...] = grad_w.reshape(gw_send.shape)
        send_gw = functools.partial(
            to_shard,
            src=lambda peer: gw_send.at[:, peer],
            dst=lambda step: gw_recv.at[step],
            kind=1,
        )
        each(shards, lambda step: send_gw(step).start())
    else:
        grad_w_ref[...] = grad_w.astype(f32)

    back = jnp.dot(dlogit, w_out_ref[...], preferred_element_type=f32)
    hidden_f = hidden.astype(f32)
    dz = back * (1.0 - hidden_f * hidden_f)
    enc_grad = dz[0:rows]
    for k in range(1, kept):
        enc_grad = enc_grad + dz[k * rows : (k + 1) * rows]
    owned_grad = lax.dot_general(
        enc_grad.astype(bf16), w_enc_ref[...], (((1,), (1,)), ((), ())), preferred_element_type=f32
    ).astype(bf16)
    outgoing[...] = (
        jnp.dot(place, owned_grad, preferred_element_type=f32)
        .astype(bf16)
        .reshape(owners, cap, width)
    )
    send_back = functools.partial(
        to_owner, src=lambda peer: outgoing.at[peer], dst=lambda step: returned.at[me], kind=1
    )
    each(owners, lambda step: send_back(step).start())
    returned[me] = outgoing[me]

    dec_grad = jnp.dot(scatter_hot, dz.astype(bf16), preferred_element_type=f32)
    gp_send[...] = (
        lax.dot_general(
            dec_grad.astype(bf16),
            w_dec_ref[...],
            (((1,), (1,)), ((), ())),
            preferred_element_type=f32,
        )
        .astype(bf16)
        .reshape(shards, lab_part, width)
    )
    send_gp = functools.partial(
        to_shard, src=lambda peer: gp_send.at[peer], dst=lambda step: gp_recv.at[step], kind=2
    )
    each(shards, lambda step: send_gp(step).start())

    if reduce_here:
        each(shards, lambda step: send_gw(step).wait())
        owner_sum = gw_send[:, part].astype(f32)
        for step in range(1, shards):
            owner_sum = owner_sum + gw_recv[step].astype(f32)
        gw2_send[...] = owner_sum.astype(bf16)
        send_gw2 = functools.partial(
            to_owner, src=lambda peer: gw2_send.at[peer], dst=lambda step: gw2_recv.at[step], kind=2
        )
        each(owners, lambda step: send_gw2(step).start())

    logp_cols = jnp.concatenate(
        [blank_logp[k * rows : (k + 1) * rows] for k in range(kept)]
        + [label_logp[k * rows : (k + 1) * rows] for k in range(kept)]
        + [jnp.zeros((rows, 8 - 2 * kept), f32)],
        axis=1,
    )
    logp_ref[...] = logp_cols.T[: 2 * kept]

    each(shards, lambda step: send_gp(step).wait())
    pred_sum = gp_send[part].astype(f32)
    for step in range(1, shards):
        pred_sum = pred_sum + gp_recv[step].astype(f32)
    grad_pred_ref[...] = pred_sum

    each(owners, lambda step: send_back(step).wait())
    grad_enc_ref[...] = jnp.dot(
        pick_t, returned[...].reshape(slots, width), preferred_element_type=f32
    ).astype(bf16)

    if reduce_here:
        each(owners, lambda step: send_gw2(step).wait())
        whole_sum = gw2_send[me].astype(f32)
        for step in range(1, owners):
            whole_sum = whole_sum + gw2_recv[step].astype(f32)
        grad_w_ref[...] = whole_sum


def shards_fn(
    enc_rows,
    dest,
    pred_rows,
    label_ids,
    block_off,
    band_start,
    w_enc,
    w_dec,
    w_out,
    bias_out,
    grad_blank,
    grad_label,
):
    owners = lax.axis_size("dp")
    shards = lax.axis_size("frame")
    rows, width = enc_rows.shape
    kept = grad_blank.shape[1]
    joint = w_enc.shape[1]
    vocab = w_out.shape[1]
    lab_part = pred_rows.shape[0]
    cap = max(TILE_ROWS, 2 * rows // owners)
    vocab_pad = -(-vocab // 128) * 128
    per_device = joint // (owners * shards)
    reduce_here = per_device % TILE_ROWS == 0
    grad_rows = per_device if reduce_here else joint
    slot_rows = per_device if reduce_here else TILE_ROWS
    slot_owners = owners if reduce_here else 1
    w_out_t = jnp.pad(w_out.T, ((0, vocab_pad - vocab), (0, 0)))
    bias = jnp.pad(bias_out, (0, vocab_pad - vocab), constant_values=MASKED)[None, :]
    bf16 = jnp.bfloat16
    vmem = pl.BlockSpec(memory_space=pltpu.VMEM)
    smem = pl.BlockSpec(memory_space=pltpu.SMEM)
    exchange = pltpu.VMEM((owners, cap, width), bf16)
    logp, grad_enc, grad_pred, grad_w = pl.pallas_call(
        functools.partial(joint_kernel, (owners, shards, cap, rows, kept, reduce_here)),
        out_shape=(
            jax.ShapeDtypeStruct((2 * kept, rows), jnp.float32),
            jax.ShapeDtypeStruct((rows, width), bf16),
            jax.ShapeDtypeStruct((lab_part, width), jnp.float32),
            jax.ShapeDtypeStruct((grad_rows, vocab_pad), jnp.float32),
        ),
        in_specs=[vmem] * 4 + [smem] + [vmem] * 7,
        out_specs=(vmem,) * 4,
        scratch_shapes=[
            exchange,
            exchange,
            exchange,
            exchange,
            pltpu.VMEM((shards, lab_part, width), bf16),
            pltpu.VMEM((slot_owners, shards, slot_rows, vocab_pad), bf16),
            pltpu.VMEM((shards, slot_owners, slot_rows, vocab_pad), bf16),
            pltpu.VMEM((slot_owners, slot_rows, vocab_pad), bf16),
            pltpu.VMEM((slot_owners, slot_rows, vocab_pad), bf16),
            pltpu.VMEM((shards, lab_part, width), bf16),
            pltpu.VMEM((shards, lab_part, width), bf16),
            pltpu.SemaphoreType.DMA((3, 2, owners)),
            pltpu.SemaphoreType.DMA((3, 2, shards)),
        ],
        compiler_params=pltpu.CompilerParams(
            collective_id=0, has_side_effects=True, vmem_limit_bytes=48 * 1024 * 1024
        ),
    )(
        enc_rows,
        dest[:, 0, :],
        pred_rows,
        label_ids,
        block_off,
        band_start[None, :],
        w_enc,
        w_dec,
        w_out_t,
        bias,
        grad_blank.T,
        grad_label.T,
    )
    if not reduce_here:
        grad_w = lax.psum_scatter(grad_w, ("dp", "frame"), scatter_dimension=0, tiled=True)
    return logp.T, grad_enc, grad_pred, grad_w[:, :vocab]


def solution(mesh):
    rows = P(("dp", "frame"), None)
    return jax.shard_map(
        shards_fn,
        mesh=mesh,
        in_specs=(
            rows,
            P(None, "frame", None),
            rows,
            P("dp", None),
            P(("dp", "frame")),
            P(("dp", "frame")),
            P(),
            P(),
            P(),
            P(),
            rows,
            rows,
        ),
        out_specs=(rows, rows, rows, rows),
        check_vma=False,
    )
```

time: 169 us -> 36 us (0.21)
  waiting for transfers between devices: 84.4 us -> 0 us
  Pallas kernels: 0 us -> 26 us
  local copies, waits for them, and re-layouts: 29.7 us -> 8.57 us
  other arithmetic: 15.9 us -> 0 us
  starting transfers between devices: 13.5 us -> 0 us
  between operations: 14.2 us -> 0.72 us
  matrix products: 5.62 us -> 0 us
  blocking collectives: 5.41 us -> 0 us
    unnamed x5 -> x0, waiting for transfers between devices: 68.5 us -> none
    pallas_call x0 -> x1, Pallas kernels: none -> 26 us  [shards_fn(): pl.pallas_call(functools.partial(joint_kernel, (owners, shards, cap, rows...]
    reduce_scatter x1 -> x0, waiting for transfers between devices: 15.9 us -> none  [shards(): lax.psum_scatter(jnp.dot(dec_grad_j, w_dec_float.T, precision=lax.Precisi...]
    gather x8 -> x0, local copies, waits for them, and re-layouts: 13.9 us -> none  [the longest x2 3.69 us: shards(): jnp.take_along_axis(logp, emitted[:, None], axis=1)[:, 0]]
    all_to_all x2 -> x0, starting transfers between devices: 13.2 us -> none  [the longest x1 7.25 us: shards(): lax.all_to_all(outbound.reshape(owners, slot_cap, feat_width), 'dp', spli...]
    scatter-add x2 -> x0, other arithmetic: 11.1 us -> none  [the longest x1 7.61 us: shards(): jax.ops.segment_sum(jnp.ones((owners * row_count,), jnp.int32), (source_i...]
    dot_general x7 -> x0, matrix products: 5.62 us -> none  [the longest x1 1.62 us: shards(): lax.dot_general(chosen, dlogit_all, (((0,), (0,)), ((), ())), preferred_e...]
    all_gather x1 -> x0, blocking collectives: 5.41 us -> none  [shards(): lax.all_gather(pred_rows, 'frame', axis=0, tiled=True)]
  transfers between devices with their start and end apart: 5 -> 0, of which waited for: 3 -> 0; matrix products, arithmetic and copies ran while one was open for 16% -> 0% of each run, Pallas kernels for 0% -> 0%
where the time goes in v1:
time: 36 us; the launch traced here: 35.2 us
  Pallas kernels  26 us (72%)
  local copies, waits for them, and re-layouts  8.57 us (24%)
  between operations  0.72 us (2%)
    pallas_call x1, Pallas kernels, shards_fn(): pl.pallas_call(functools.partial(joint_kernel, (owners, shards, cap, rows...  26 us
    unnamed x26, local copies, waits for them, and re-layouts  7.48 us
    pad x1, local copies, waits for them, and re-layouts, shards_fn(): w_out_t = jnp.pad(w_out.T, ((0, vocab_pad - vocab), (0, 0)))  1.09 us

profile of v1, /device:TPU:0, one launch (start us, length us, event | category | flops | bytes accessed | tf_op | source)
XLA Modules:
  0.0 35.2 jit_solution(3079617592415651374)
XLA Ops:
  0.6 0.0 copy-start.10
  0.6 0.0 copy-start.4
  0.7 0.0 copy-start
  0.7 0.0 copy-start.1
  0.7 0.6 %copy-done.10 = f32[500]{0:T(512)S(1)} copy-done((f32[500]{0:T(512)S(1)}, f32[500]{0:T(512)}, u32[]{:S(2)}) %copy-start.10) | copy-done | bytes 2024
  1.3 0.0 copy-start.7
  1.3 1.1 %pad.8.w_out_ref = bf16[512,512]{1,0:T(8,128)(2,1)S(1)} pad(bf16[500,512]{1,0:T(8,128)(2,1)} %bitcast.15, bf16[]{:T(256)} %constant.1.clone.1), padding=0_12x0_0 | pad | bytes 1036290 | tf_op jit(solution)/shard_map/jit(_pad)/pad | solution.py:343
  2.4 0.0 copy-done.4
  2.4 0.0 copy-done
  2.4 0.0 copy-done.1
  2.4 0.0 copy-done.7
  2.5 0.0 copy-start.2
  2.5 0.9 %copy-done.2 = bf16[128,512]{1,0:T(8,128)(2,1)S(1)} copy-done((bf16[128,512]{1,0:T(8,128)(2,1)S(1)}, bf16[128,512]{1,0:T(8,128)(2,1)}, u32[]{:S(2)}) %copy-start.2) | copy-done | bytes 131096
  3.4 0.0 copy-start.3
  3.4 0.8 %copy-done.3 = bf16[32,512]{1,0:T(8,128)(2,1)S(1)} copy-done((bf16[32,512]{1,0:T(8,128)(2,1)S(1)}, bf16[32,512]{1,0:T(8,128)(2,1)}, u32[]{:S(2)}) %copy-start.3) | copy-done | bytes 32792
  4.1 0.0 copy-start.5
  4.1 0.7 %copy-done.5 = f32[128,3]{0,1:T(4,128)S(1)} copy-done((f32[128,3]{0,1:T(4,128)S(1)}, f32[128,3]{0,1:T(4,128)}, u32[]{:S(2)}) %copy-start.5) | copy-done | bytes 1560
  4.8 0.0 copy-start.6
  4.8 0.7 %copy-done.6 = f32[128,3]{0,1:T(4,128)S(1)} copy-done((f32[128,3]{0,1:T(4,128)S(1)}, f32[128,3]{0,1:T(4,128)}, u32[]{:S(2)}) %copy-start.6) | copy-done | bytes 1560
  5.5 0.0 copy-start.8
  5.5 0.7 %copy-done.8 = s32[2]{0:T(128)S(1)} copy-done((s32[2]{0:T(128)S(1)}, s32[2]{0:T(128)}, u32[]{:S(2)}) %copy-start.8) | copy-done | bytes 32
  6.1 0.0 copy-start.9
  6.1 0.7 %copy-done.9 = s32[128]{0:T(128)S(1)} copy-done((s32[128]{0:T(128)S(1)}, s32[128]{0:T(128)}, u32[]{:S(2)}) %copy-start.9) | copy-done | bytes 536
  6.8 26.0 %shard_map.147 = (f32[6,128]{1,0:T(8,128)S(1)}, bf16[128,512]{1,0:T(8,128)(2,1)S(1)}, f32[32,512]{1,0:T(8,128)S(1)}, f32[16,512]{1,0:T(8,128)S(1)}) custom-call(bf16[128,512]{1,0:T(8,128)(2,1)S(1)} %copy-done.2, s32[8,128]{1,0:T(8,128)S(1)} %bitcast.10, bf16[32,512]{1,0:T(8,128)(2,1)S(1)} %copy-done.3, s32[1,128]{1,0:T(1,128)S(1)} %copy-done.7, ...), custom_call_target="tpu_custom_call" | custom-call | tf_op jit(solution)/shard_map/pallas_call | solution.py:349
  32.8 0.6 %copy.20 = f32[128,6]{0,1:T(8,128)} copy(f32[128,6]{0,1:T(8,128)S(1)} %bitcast.11) | data formatting | bytes 6144
  33.4 0.7 %copy.21 = bf16[128,512]{1,0:T(8,128)(2,1)} copy(bf16[128,512]{1,0:T(8,128)(2,1)S(1)} %get-tuple-element.17) | data formatting | bytes 262144
  34.0 0.6 %copy.22 = f32[32,512]{1,0:T(8,128)} copy(f32[32,512]{1,0:T(8,128)S(1)} %get-tuple-element.18) | data formatting | bytes 131072
  34.6 0.6 %copy.23 = f32[16,500]{1,0:T(8,128)} copy(f32[16,500]{1,0:T(8,128)S(1)} %bitcast.8) | data formatting | bytes 64000
  (1 shorter events, 0.0 us)
Async XLA Ops:
  0.6 0.7 %copy-start.10 = (f32[500]{0:T(512)S(1)}, f32[500]{0:T(512)}, u32[]{:S(2)}) copy-start(f32[500]{0:T(512)} %param.21) | copy-start | bytes 6004
  0.6 1.8 %copy-start.4 = (s32[8,1,128]{2,1,0:T(1,128)S(1)}, s32[8,1,128]{2,1,0:T(1,128)}, u32[]{:S(2)}) copy-start(s32[8,1,128]{2,1,0:T(1,128)} %param.13) | copy-start | bytes 12292
  0.7 1.8 %copy-start = (bf16[512,512]{1,0:T(8,128)(2,1)S(1)}, bf16[512,512]{1,0:T(8,128)(2,1)}, u32[]{:S(2)}) copy-start(bf16[512,512]{1,0:T(8,128)(2,1)} %w_enc_ref.1) | copy-start | bytes 1572868
  0.7 1.8 %copy-start.1 = (bf16[512,512]{1,0:T(8,128)(2,1)S(1)}, bf16[512,512]{1,0:T(8,128)(2,1)}, u32[]{:S(2)}) copy-start(bf16[512,512]{1,0:T(8,128)(2,1)} %w_dec_ref.1) | copy-start | bytes 1572868
  1.3 1.1 %copy-start.7 = (s32[1,128]{1,0:T(1,128)S(1)}, s32[1,128]{1,0:T(1,128)}, u32[]{:S(2)}) copy-start(s32[1,128]{1,0:T(1,128)} %label_ref.1) | copy-start | bytes 1540
  2.5 0.9 %copy-start.2 = (bf16[128,512]{1,0:T(8,128)(2,1)S(1)}, bf16[128,512]{1,0:T(8,128)(2,1)}, u32[]{:S(2)}) copy-start(bf16[128,512]{1,0:T(8,128)(2,1)} %enc_ref.1) | copy-start | bytes 393220
  3.4 0.8 %copy-start.3 = (bf16[32,512]{1,0:T(8,128)(2,1)S(1)}, bf16[32,512]{1,0:T(8,128)(2,1)}, u32[]{:S(2)}) copy-start(bf16[32,512]{1,0:T(8,128)(2,1)} %pred_ref.1) | copy-start | bytes 98308
  4.1 0.7 %copy-start.5 = (f32[128,3]{0,1:T(4,128)S(1)}, f32[128,3]{0,1:T(4,128)}, u32[]{:S(2)}) copy-start(f32[128,3]{0,1:T(4,128)} %param.22) | copy-start | bytes 4612
  4.8 0.7 %copy-start.6 = (f32[128,3]{0,1:T(4,128)S(1)}, f32[128,3]{0,1:T(4,128)}, u32[]{:S(2)}) copy-start(f32[128,3]{0,1:T(4,128)} %param.23) | copy-start | bytes 4612
  5.5 0.7 %copy-start.8 = (s32[2]{0:T(128)S(1)}, s32[2]{0:T(128)}, u32[]{:S(2)}) copy-start(s32[2]{0:T(128)} %off_ref.1) | copy-start | bytes 28
  6.1 0.7 %copy-start.9 = (s32[128]{0:T(128)S(1)}, s32[128]{0:T(128)}, u32[]{:S(2)}) copy-start(s32[128]{0:T(128)} %param.17) | copy-start | bytes 1540

commit v2 on v1

--- a/solution.py
+++ b/solution.py
@@ -9,7 +9,7 @@
 
 BLOCK = 64
 TILE_ROWS = 16
-MASKED = -1e30
+VMEM_BYTES = 64 * 1024 * 1024
 MESH = pl.DeviceIdType.MESH
 
 
@@ -20,9 +20,35 @@
 
 def joint_kernel(
     dims,
+    enc_hbm,
+    dest_hbm,
+    pred_ref,
+    label_hbm,
+    off_hbm,
+    band_hbm,
+    w_enc_hbm,
+    w_dec_hbm,
+    w_out_hbm,
+    bias_hbm,
+    blank_hbm,
+    cot_hbm,
+    logp_hbm,
+    grad_enc_hbm,
+    grad_pred_hbm,
+    grad_w_hbm,
+    outbound,
+    arrived,
+    outgoing,
+    returned,
+    pred_all,
+    gw_send,
+    gw_recv,
+    gw2_send,
+    gw2_recv,
+    gp_send,
+    gp_recv,
     enc_ref,
     dest_ref,
-    pred_ref,
     label_ref,
     off_ref,
     band_ref,
@@ -36,26 +62,16 @@
     grad_enc_ref,
     grad_pred_ref,
     grad_w_ref,
-    outbound,
-    arrived,
-    outgoing,
-    returned,
-    pred_all,
-    gw_send,
-    gw_recv,
-    gw2_send,
-    gw2_recv,
-    gp_send,
-    gp_recv,
     dp_sem,
     frame_sem,
+    load_sem,
+    store_sem,
 ):
     owners, shards, cap, rows, kept, reduce_here = dims
     me = lax.axis_index("dp")
     part = lax.axis_index("frame")
-    width = enc_ref.shape[1]
-    joint = w_enc_ref.shape[1]
-    vocab = w_out_ref.shape[0]
+    width = enc_hbm.shape[1]
+    vocab = w_out_hbm.shape[0]
     lab_part = pred_ref.shape[0]
     labels = shards * lab_part
     slots = owners * cap
@@ -88,7 +104,7 @@
 
     def each(count, act):
         if count <= 8:
-            for step in range(1, count):
+            for step in sorted(range(1, count), key=lambda step: abs(2 * step - count)):
                 act(step)
         else:
 
@@ -98,6 +114,18 @@
 
             lax.fori_loop(1, count, body, 0)
 
+    stores = [
+        pltpu.make_async_copy(src, dst, store_sem.at[slot])
+        for slot, (src, dst) in enumerate(
+            [
+                (logp_ref, logp_hbm),
+                (grad_pred_ref, grad_pred_hbm),
+                (grad_enc_ref, grad_enc_hbm),
+                (grad_w_ref, grad_w_hbm),
+            ]
+        )
+    ]
+
     barrier = pltpu.get_barrier_semaphore()
 
     def greet_owner(step):
@@ -112,6 +140,27 @@
 
     each(owners, greet_owner)
     each(shards, greet_shard)
+
+    pairs = [
+        (dest_hbm, dest_ref),
+        (enc_hbm, enc_ref),
+        (off_hbm, off_ref),
+        (band_hbm, band_ref),
+        (blank_hbm, blank_ref),
+        (cot_hbm, cot_ref),
+        (label_hbm, label_ref),
+        (pred_ref, pred_all.at[part]),
+        (w_dec_hbm, w_dec_ref),
+        (w_enc_hbm, w_enc_ref),
+        (w_out_hbm, w_out_ref),
+        (bias_hbm, bias_ref),
+    ]
+    loads = [
+        pltpu.make_async_copy(src, dst, load_sem.at[slot]) for slot, (src, dst) in enumerate(pairs)
+    ]
+    for load in loads:
+        load.start()
+    loads[0].wait()
 
     shape = (slots, rows)
     slot_owner = lax.shift_right_logical(iota(shape, 0), log2(cap))
@@ -139,6 +188,7 @@
     pick = (my_dest == slot_owner * rows + out_row) & (out_row < rows)
     pick = jnp.where(pick, 1.0, 0.0)
     place = jnp.where(lane == in_row, 1.0, 0.0)
+    loads[1].wait()
     out_rows = jnp.dot(pick.astype(bf16), enc_ref[...], preferred_element_type=f32).astype(bf16)
     outbound[...] = out_rows.reshape(owners, cap, width)
 
@@ -153,7 +203,8 @@
     each(owners, lambda step: send_enc(step).start())
     each(shards, lambda step: send_pred(step).start())
     arrived[me] = outbound[me]
-    pred_all[part] = pred_ref[...]
+    for load in loads[2:8]:
+        load.wait()
 
     half = iota((1, rows), 1) // BLOCK
     base_row = band_ref[...]
@@ -190,11 +241,14 @@
     place = place.astype(bf16)
 
     each(shards, lambda step: send_pred(step).wait())
+    loads[8].wait()
     dec_joint = jnp.dot(
         pred_all[...].reshape(labels, width), w_dec_ref[...], preferred_element_type=f32
     ).astype(bf16)
     dec_rows = jnp.dot(gather_hot.astype(bf16), dec_joint, preferred_element_type=f32)
 
+    for load in loads[9:]:
+        load.wait()
     each(owners, lambda step: send_enc(step).wait())
     enc_owned = jnp.dot(
         place_t, arrived[...].reshape(slots, width), preferred_element_type=f32
@@ -237,6 +291,7 @@
         each(shards, lambda step: send_gw(step).start())
     else:
         grad_w_ref[...] = grad_w.astype(f32)
+        stores[3].start()
 
     back = jnp.dot(dlogit, w_out_ref[...], preferred_element_type=f32)
     hidden_f = hidden.astype(f32)
@@ -292,17 +347,20 @@
         axis=1,
     )
     logp_ref[...] = logp_cols.T[: 2 * kept]
+    stores[0].start()
 
     each(shards, lambda step: send_gp(step).wait())
     pred_sum = gp_send[part].astype(f32)
     for step in range(1, shards):
         pred_sum = pred_sum + gp_recv[step].astype(f32)
     grad_pred_ref[...] = pred_sum
+    stores[1].start()
 
     each(owners, lambda step: send_back(step).wait())
     grad_enc_ref[...] = jnp.dot(
         pick_t, returned[...].reshape(slots, width), preferred_element_type=f32
     ).astype(bf16)
+    stores[2].start()
 
     if reduce_here:
         each(owners, lambda step: send_gw2(step).wait())
@@ -310,6 +368,21 @@
         for step in range(1, owners):
             whole_sum = whole_sum + gw2_recv[step].astype(f32)
         grad_w_ref[...] = whole_sum
+        stores[3].start()
+    for store in stores:
+        store.wait()
+
+
+def finish_kernel(*refs):
+    *ends, sem = refs
+    count = len(ends) // 2
+    copies = [
+        pltpu.make_async_copy(ends[slot], ends[count + slot], sem.at[slot]) for slot in range(count)
+    ]
+    for copy in copies:
+        copy.start()
+    for copy in copies:
+        copy.wait()
 
 
 def shards_fn(
@@ -334,47 +407,15 @@
     vocab = w_out.shape[1]
     lab_part = pred_rows.shape[0]
     cap = max(TILE_ROWS, 2 * rows // owners)
-    vocab_pad = -(-vocab // 128) * 128
     per_device = joint // (owners * shards)
     reduce_here = per_device % TILE_ROWS == 0
     grad_rows = per_device if reduce_here else joint
     slot_rows = per_device if reduce_here else TILE_ROWS
     slot_owners = owners if reduce_here else 1
-    w_out_t = jnp.pad(w_out.T, ((0, vocab_pad - vocab), (0, 0)))
-    bias = jnp.pad(bias_out, (0, vocab_pad - vocab), constant_values=MASKED)[None, :]
     bf16 = jnp.bfloat16
-    vmem = pl.BlockSpec(memory_space=pltpu.VMEM)
-    smem = pl.BlockSpec(memory_space=pltpu.SMEM)
+    hbm = pl.BlockSpec(memory_space=pltpu.HBM)
     exchange = pltpu.VMEM((owners, cap, width), bf16)
-    logp, grad_enc, grad_pred, grad_w = pl.pallas_call(
-        functools.partial(joint_kernel, (owners, shards, cap, rows, kept, reduce_here)),
-        out_shape=(
-            jax.ShapeDtypeStruct((2 * kept, rows), jnp.float32),
-            jax.ShapeDtypeStruct((rows, width), bf16),
-            jax.ShapeDtypeStruct((lab_part, width), jnp.float32),
-            jax.ShapeDtypeStruct((grad_rows, vocab_pad), jnp.float32),
-        ),
-        in_specs=[vmem] * 4 + [smem] + [vmem] * 7,
-        out_specs=(vmem,) * 4,
-        scratch_shapes=[
-            exchange,
-            exchange,
-            exchange,
-            exchange,
-            pltpu.VMEM((shards, lab_part, width), bf16),
-            pltpu.VMEM((slot_owners, shards, slot_rows, vocab_pad), bf16),
-            pltpu.VMEM((shards, slot_owners, slot_rows, vocab_pad), bf16),
-            pltpu.VMEM((slot_owners, slot_rows, vocab_pad), bf16),
-            pltpu.VMEM((slot_owners, slot_rows, vocab_pad), bf16),
-            pltpu.VMEM((shards, lab_part, width), bf16),
-            pltpu.VMEM((shards, lab_part, width), bf16),
-            pltpu.SemaphoreType.DMA((3, 2, owners)),
-            pltpu.SemaphoreType.DMA((3, 2, shards)),
-        ],
-        compiler_params=pltpu.CompilerParams(
-            collective_id=0, has_side_effects=True, vmem_limit_bytes=48 * 1024 * 1024
-        ),
-    )(
+    arrays = (
         enc_rows,
         dest[:, 0, :],
         pred_rows,
@@ -383,14 +424,63 @@
         band_start[None, :],
         w_enc,
         w_dec,
-        w_out_t,
-        bias,
+        w_out.T,
+        bias_out[None, :],
         grad_blank.T,
         grad_label.T,
     )
+    fetched = [
+        (pltpu.SMEM if slot == 4 else pltpu.VMEM)(array.shape, array.dtype)
+        for slot, array in enumerate(arrays)
+        if slot != 2
+    ]
+    outputs = (
+        jax.ShapeDtypeStruct((2 * kept, rows), jnp.float32),
+        jax.ShapeDtypeStruct((rows, width), bf16),
+        jax.ShapeDtypeStruct((lab_part, width), jnp.float32),
+        jax.ShapeDtypeStruct((grad_rows, vocab), jnp.float32),
+    )
+    results = pl.pallas_call(
+        functools.partial(joint_kernel, (owners, shards, cap, rows, kept, reduce_here)),
+        out_shape=outputs,
+        in_specs=[hbm] * len(arrays),
+        out_specs=(hbm,) * 4,
+        scratch_shapes=[
+            exchange,
+            exchange,
+            exchange,
+            exchange,
+            pltpu.VMEM((shards, lab_part, width), bf16),
+            pltpu.VMEM((slot_owners, shards, slot_rows, vocab), bf16),
+            pltpu.VMEM((shards, slot_owners, slot_rows, vocab), bf16),
+            pltpu.VMEM((slot_owners, slot_rows, vocab), bf16),
+            pltpu.VMEM((slot_owners, slot_rows, vocab), bf16),
+            pltpu.VMEM((shards, lab_part, width), bf16),
+            pltpu.VMEM((shards, lab_part, width), bf16),
+            *fetched,
+            *(pltpu.VMEM(output.shape, output.dtype) for output in outputs),
+            pltpu.SemaphoreType.DMA((3, 2, owners)),
+            pltpu.SemaphoreType.DMA((3, 2, shards)),
+            pltpu.SemaphoreType.DMA((len(arrays),)),
+            pltpu.SemaphoreType.DMA((len(outputs),)),
+        ],
+        compiler_params=pltpu.CompilerParams(
+            collective_id=0, has_side_effects=True, vmem_limit_bytes=VMEM_BYTES
+        ),
+    )(*arrays)
+    tail = ()
     if not reduce_here:
-        grad_w = lax.psum_scatter(grad_w, ("dp", "frame"), scatter_dimension=0, tiled=True)
-    return logp.T, grad_enc, grad_pred, grad_w[:, :vocab]
+        *results, grad_w = results
+        tail = (lax.psum_scatter(grad_w, ("dp", "frame"), scatter_dimension=0, tiled=True),)
+    logp, *others = pl.pallas_call(
+        finish_kernel,
+        out_shape=tuple(jax.ShapeDtypeStruct(array.shape, array.dtype) for array in results),
+        in_specs=[hbm] * len(results),
+        out_specs=(hbm,) * len(results),
+        scratch_shapes=[pltpu.SemaphoreType.DMA((len(results),))],
+        compiler_params=pltpu.CompilerParams(vmem_limit_bytes=VMEM_BYTES),
+    )(*results)
+    return (logp.T, *others, *tail)
 
 
 def solution(mesh):

time: 36 us -> 36.6 us (1.017); the launches traced: 35.2 us -> 36.2 us
  Pallas kernels: 26 us -> 35.6 us
  local copies, waits for them, and re-layouts: 8.57 us -> 0 us
    pallas_call x0 -> x1, Pallas kernels: none -> 8.18 us  [shards_fn(): pl.pallas_call(finish_kernel, out_shape=tuple((jax.ShapeDtypeStruct(array...]
    unnamed x26 -> x0, local copies, waits for them, and re-layouts: 7.48 us -> none
    pallas_call x1, Pallas kernels: 26 us -> 27.4 us  [shards_fn(): pl.pallas_call(functools.partial(joint_kernel, (owners, shards, cap, rows...]
    pad x2 -> x0, local copies, waits for them, and re-layouts: 1.09 us -> none  [the longest x1 1.09 us: shards_fn(): w_out_t = jnp.pad(w_out.T, ((0, vocab_pad - vocab), (0, 0)))]
where the time goes in v2:
time: 36.6 us; the launch traced here: 36.2 us
  Pallas kernels  35.6 us (97%)
  between operations  0.64 us (2%)
    pallas_call x1, Pallas kernels, shards_fn(): pl.pallas_call(functools.partial(joint_kernel, (owners, shards, cap, rows...  27.4 us
    pallas_call x1, Pallas kernels, shards_fn(): pl.pallas_call(finish_kernel, out_shape=tuple((jax.ShapeDtypeStruct(array...  8.18 us

profile of v2, /device:TPU:0, one launch (start us, length us, event | category | flops | bytes accessed | tf_op | source)
XLA Modules:
  0.0 36.2 jit_solution(7617935258384205231)
XLA Ops:
  0.6 27.4 %shard_map.147 = (f32[6,128]{1,0:T(8,128)}, bf16[128,512]{1,0:T(8,128)(2,1)}, f32[32,512]{1,0:T(8,128)}, f32[16,500]{1,0:T(8,128)}) custom-call(bf16[128,512]{1,0:T(8,128)(2,1)} %enc_hbm.1, s32[8,128]{1,0:T(8,128)} %bitcast.8, bf16[32,512]{1,0:T(8,128)(2,1)} %pred_ref.1, s32[1,128]{1,0:T(1,128)} %label_hbm.1, s32[2]{0:T(128)} %off_hbm.1, s32[1,128]{1,0:T(1,128)} %bitcast.12, ...), custom_call_target="tpu_custom_call" | custom-call | tf_op jit(solution)/shard_map/pallas_call | solution.py:443
  28.0 8.2 %shard_map.148 = (f32[6,128]{1,0:T(8,128)}, bf16[128,512]{1,0:T(8,128)(2,1)}, f32[32,512]{1,0:T(8,128)}, f32[16,500]{1,0:T(8,128)}) custom-call(f32[6,128]{1,0:T(8,128)} %get-tuple-element.12.refs_0_, bf16[128,512]{1,0:T(8,128)(2,1)} %get-tuple-element.13.refs_1_, f32[32,512]{1,0:T(8,128)} %get-tuple-element.14.refs_2_, f32[16,500]{1,0:T(8,128)} %get-tuple-element.15.refs_3_), custom_call_target="tpu_custom_call" | custom-call | tf_op jit(solution)/shard_map/pallas_call | solution.py:475

commit v3 on v2

--- a/solution.py
+++ b/solution.py
@@ -41,10 +41,14 @@
     outgoing,
     returned,
     pred_all,
-    gw_send,
-    gw_recv,
-    gw2_send,
-    gw2_recv,
+    core_send,
+    core_recv,
+    core_sum,
+    first_recv,
+    first_sum,
+    second_recv,
+    last_sum,
+    last_recv,
     gp_send,
     gp_recv,
     enc_ref,
@@ -64,6 +68,7 @@
     grad_w_ref,
     dp_sem,
     frame_sem,
+    sum_sem,
     load_sem,
     store_sem,
 ):
@@ -280,15 +285,31 @@
     grad_w = lax.dot_general(
         hidden, dlogit, (((0,), (0,)), ((), ())), preferred_element_type=f32
     ).astype(bf16)
+    inner, core = lax.rem(me, 2), lax.rem(part, 2)
+    outer_at, y = me // 2, part // 2
+    outer = owners // 2
+    half = outer // 2
+    other_core = {"frame": part + 1 - 2 * core}
+    other_y = {"frame": lax.rem(part + 2, shards)}
+    other_x = {"dp": me + 1 - 2 * inner}
+
+    def send_sum(slot, src, dst, device):
+        return pltpu.make_async_remote_copy(
+            src_ref=src,
+            dst_ref=dst,
+            send_sem=sum_sem.at[0, slot],
+            recv_sem=sum_sem.at[1, slot],
+            device_id=device,
+            device_id_type=MESH,
+        )
+
+    def add(one, two):
+        return (one.astype(f32) + two.astype(f32)).astype(bf16)
+
     if reduce_here:
-        gw_send[...] = grad_w.reshape(gw_send.shape)
-        send_gw = functools.partial(
-            to_shard,
-            src=lambda peer: gw_send.at[:, peer],
-            dst=lambda step: gw_recv.at[step],
-            kind=1,
-        )
-        each(shards, lambda step: send_gw(step).start())
+        core_send[...] = grad_w.reshape(core_send.shape)
+        core_step = send_sum(0, core_send.at[:, :, :, 1 - core], core_recv, other_core)
+        core_step.start()
     else:
         grad_w_ref[...] = grad_w.astype(f32)
         stores[3].start()
@@ -313,6 +334,17 @@
     each(owners, lambda step: send_back(step).start())
     returned[me] = outgoing[me]
 
+    if reduce_here:
+        core_step.wait()
+        core_sum[...] = add(core_send[:, :, :, core], core_recv[...])
+        low, high = pl.ds(0, half), pl.ds(half, half)
+        first_steps = (
+            send_sum(1, core_sum.at[low, :, 1 - y], first_recv.at[0], other_y),
+            send_sum(2, core_sum.at[high, 1 - inner], first_recv.at[1], other_x),
+        )
+        for step in first_steps:
+            step.start()
+
     dec_grad = jnp.dot(scatter_hot, dz.astype(bf16), preferred_element_type=f32)
     gp_send[...] = (
         lax.dot_general(
@@ -325,20 +357,21 @@
         .reshape(shards, lab_part, width)
     )
     send_gp = functools.partial(
-        to_shard, src=lambda peer: gp_send.at[peer], dst=lambda step: gp_recv.at[step], kind=2
+        to_shard, src=lambda peer: gp_send.at[peer], dst=lambda step: gp_recv.at[step], kind=1
     )
     each(shards, lambda step: send_gp(step).start())
 
     if reduce_here:
-        each(shards, lambda step: send_gw(step).wait())
-        owner_sum = gw_send[:, part].astype(f32)
-        for step in range(1, shards):
-            owner_sum = owner_sum + gw_recv[step].astype(f32)
-        gw2_send[...] = owner_sum.astype(bf16)
-        send_gw2 = functools.partial(
-            to_owner, src=lambda peer: gw2_send.at[peer], dst=lambda step: gw2_recv.at[step], kind=2
-        )
-        each(owners, lambda step: send_gw2(step).start())
+        for step in first_steps:
+            step.wait()
+        first_sum[0] = add(core_sum[low, :, y], first_recv[0])
+        first_sum[1] = add(core_sum[high, inner], first_recv[1])
+        second_steps = (
+            send_sum(3, first_sum.at[0, :, 1 - inner], second_recv.at[0], other_x),
+            send_sum(4, first_sum.at[1, :, 1 - y], second_recv.at[1], other_y),
+        )
+        for step in second_steps:
+            step.start()
 
     logp_cols = jnp.concatenate(
         [blank_logp[k * rows : (k + 1) * rows] for k in range(kept)]
@@ -348,6 +381,22 @@
     )
     logp_ref[...] = logp_cols.T[: 2 * kept]
     stores[0].start()
+
+    if reduce_here:
+        for step in second_steps:
+            step.wait()
+        last_sum[low] = add(first_sum[0, :, inner], second_recv[0])
+        last_sum[high] = add(first_sum[1, :, y], second_recv[1])
+        last_steps = []
+        for step in range(1, outer):
+            peer = lax.rem(outer_at + step, outer)
+            last_steps.append(
+                send_sum(
+                    4 + step, last_sum.at[peer], last_recv.at[step], {"dp": 2 * peer + inner}
+                )
+            )
+        for step in last_steps:
+            step.start()
 
     each(shards, lambda step: send_gp(step).wait())
     pred_sum = gp_send[part].astype(f32)
@@ -363,10 +412,11 @@
     stores[2].start()
 
     if reduce_here:
-        each(owners, lambda step: send_gw2(step).wait())
-        whole_sum = gw2_send[me].astype(f32)
-        for step in range(1, owners):
-            whole_sum = whole_sum + gw2_recv[step].astype(f32)
+        for step in last_steps:
+            step.wait()
+        whole_sum = last_sum[outer_at].astype(f32)
+        for step in range(1, outer):
+            whole_sum = whole_sum + last_recv[step].astype(f32)
         grad_w_ref[...] = whole_sum
         stores[3].start()
     for store in stores:
@@ -374,15 +424,24 @@
 
 
 def finish_kernel(*refs):
-    *ends, sem = refs
-    count = len(ends) // 2
-    copies = [
-        pltpu.make_async_copy(ends[slot], ends[count + slot], sem.at[slot]) for slot in range(count)
+    *ends, load_sem, store_sem = refs
+    count = len(ends) // 3
+    sources, results, held = ends[:count], ends[count : 2 * count], ends[2 * count :]
+    loads = [
+        pltpu.make_async_copy(sources[slot], held[slot], load_sem.at[slot])
+        for slot in range(count)
     ]
-    for copy in copies:
-        copy.start()
-    for copy in copies:
-        copy.wait()
+    stores = [
+        pltpu.make_async_copy(held[slot], results[slot], store_sem.at[slot])
+        for slot in range(count)
+    ]
+    for load in loads:
+        load.start()
+    for load, store in zip(loads, stores):
+        load.wait()
+        store.start()
+    for store in stores:
+        store.wait()
 
 
 def shards_fn(
@@ -408,10 +467,11 @@
     lab_part = pred_rows.shape[0]
     cap = max(TILE_ROWS, 2 * rows // owners)
     per_device = joint // (owners * shards)
-    reduce_here = per_device % TILE_ROWS == 0
+    reduce_here = per_device % TILE_ROWS == 0 and owners % 4 == 0 and shards == 4
     grad_rows = per_device if reduce_here else joint
     slot_rows = per_device if reduce_here else TILE_ROWS
-    slot_owners = owners if reduce_here else 1
+    outer = owners // 2 if reduce_here else 2
+    half = outer // 2
     bf16 = jnp.bfloat16
     hbm = pl.BlockSpec(memory_space=pltpu.HBM)
     exchange = pltpu.VMEM((owners, cap, width), bf16)
@@ -451,16 +511,21 @@
             exchange,
             exchange,
             pltpu.VMEM((shards, lab_part, width), bf16),
-            pltpu.VMEM((slot_owners, shards, slot_rows, vocab), bf16),
-            pltpu.VMEM((shards, slot_owners, slot_rows, vocab), bf16),
-            pltpu.VMEM((slot_owners, slot_rows, vocab), bf16),
-            pltpu.VMEM((slot_owners, slot_rows, vocab), bf16),
+            pltpu.VMEM((outer, 2, 2, 2, slot_rows, vocab), bf16),
+            pltpu.VMEM((outer, 2, 2, slot_rows, vocab), bf16),
+            pltpu.VMEM((outer, 2, 2, slot_rows, vocab), bf16),
+            pltpu.VMEM((2, half, 2, slot_rows, vocab), bf16),
+            pltpu.VMEM((2, half, 2, slot_rows, vocab), bf16),
+            pltpu.VMEM((2, half, slot_rows, vocab), bf16),
+            pltpu.VMEM((outer, slot_rows, vocab), bf16),
+            pltpu.VMEM((outer, slot_rows, vocab), bf16),
             pltpu.VMEM((shards, lab_part, width), bf16),
             pltpu.VMEM((shards, lab_part, width), bf16),
             *fetched,
             *(pltpu.VMEM(output.shape, output.dtype) for output in outputs),
-            pltpu.SemaphoreType.DMA((3, 2, owners)),
-            pltpu.SemaphoreType.DMA((3, 2, shards)),
+            pltpu.SemaphoreType.DMA((2, 2, owners)),
+            pltpu.SemaphoreType.DMA((2, 2, shards)),
+            pltpu.SemaphoreType.DMA((2, 5 + outer)),
             pltpu.SemaphoreType.DMA((len(arrays),)),
             pltpu.SemaphoreType.DMA((len(outputs),)),
         ],
@@ -477,7 +542,11 @@
         out_shape=tuple(jax.ShapeDtypeStruct(array.shape, array.dtype) for array in results),
         in_specs=[hbm] * len(results),
         out_specs=(hbm,) * len(results),
-        scratch_shapes=[pltpu.SemaphoreType.DMA((len(results),))],
+        scratch_shapes=[
+            *(pltpu.VMEM(array.shape, array.dtype) for array in results),
+            pltpu.SemaphoreType.DMA((len(results),)),
+            pltpu.SemaphoreType.DMA((len(results),)),
+        ],
         compiler_params=pltpu.CompilerParams(vmem_limit_bytes=VMEM_BYTES),
     )(*results)
     return (logp.T, *others, *tail)

time: 36.6 us -> 31.6 us (0.86)
  Pallas kernels: 35.6 us -> 30.7 us
    pallas_call x1, Pallas kernels: 8.18 us -> 1.66 us  [shards_fn(): pl.pallas_call(finish_kernel, out_shape=tuple((jax.ShapeDtypeStruct(array...]
    pallas_call x1, Pallas kernels: 27.4 us -> 29.1 us  [shards_fn(): pl.pallas_call(functools.partial(joint_kernel, (owners, shards, cap, rows...]
where the time goes in v3:
time: 31.6 us; the launch traced here: 31.4 us
  Pallas kernels  30.7 us (97%)
  between operations  0.64 us (2%)
    pallas_call x1, Pallas kernels, shards_fn(): pl.pallas_call(functools.partial(joint_kernel, (owners, shards, cap, rows...  29.1 us
    pallas_call x1, Pallas kernels, shards_fn(): pl.pallas_call(finish_kernel, out_shape=tuple((jax.ShapeDtypeStruct(array...  1.66 us

profile of v3, /device:TPU:0, one launch (start us, length us, event | category | flops | bytes accessed | tf_op | source)
XLA Modules:
  0.0 31.4 jit_solution(5532309613111089005)
XLA Ops:
  0.6 29.1 %shard_map.147 = (f32[6,128]{1,0:T(8,128)}, bf16[128,512]{1,0:T(8,128)(2,1)}, f32[32,512]{1,0:T(8,128)}, f32[16,500]{1,0:T(8,128)}) custom-call(bf16[128,512]{1,0:T(8,128)(2,1)} %enc_hbm.1, s32[8,128]{1,0:T(8,128)} %bitcast.8, bf16[32,512]{1,0:T(8,128)(2,1)} %pred_ref.1, s32[1,128]{1,0:T(1,128)} %label_hbm.1, s32[2]{0:T(128)} %off_hbm.1, s32[1,128]{1,0:T(1,128)} %bitcast.12, ...), custom_call_target="tpu_custom_call" | custom-call | tf_op jit(solution)/shard_map/pallas_call | solution.py:503
  29.7 1.7 %shard_map.148 = (f32[6,128]{1,0:T(8,128)}, bf16[128,512]{1,0:T(8,128)(2,1)}, f32[32,512]{1,0:T(8,128)}, f32[16,500]{1,0:T(8,128)}) custom-call(f32[6,128]{1,0:T(8,128)} %get-tuple-element.12.refs_0_, bf16[128,512]{1,0:T(8,128)(2,1)} %get-tuple-element.13.refs_1_, f32[32,512]{1,0:T(8,128)} %get-tuple-element.14.refs_2_, f32[16,500]{1,0:T(8,128)} %get-tuple-element.15.refs_3_), custom_call_target="tpu_custom_call" | custom-call | tf_op jit(solution)/shard_map/pallas_call | solution.py:540

commit v4 on v3

--- a/solution.py
+++ b/solution.py
@@ -62,6 +62,9 @@
     bias_ref,
     blank_ref,
     cot_ref,
+    w_out_t,
+    w_enc_t,
+    w_dec_t,
     logp_ref,
     grad_enc_ref,
     grad_pred_ref,
@@ -254,36 +257,46 @@
 
     for load in loads[9:]:
         load.wait()
+    w_out_t[...] = w_out_ref[...].T
+    w_enc_t[...] = w_enc_ref[...].T
+    w_dec_t[...] = w_dec_ref[...].T
     each(owners, lambda step: send_enc(step).wait())
     enc_owned = jnp.dot(
         place_t, arrived[...].reshape(slots, width), preferred_element_type=f32
     ).astype(bf16)
     enc_joint = jnp.dot(enc_owned, w_enc_ref[...], preferred_element_type=f32)
-    hidden = jnp.tanh(jnp.concatenate([enc_joint] * kept, axis=0) + dec_rows).astype(bf16)
-    logits = (
-        lax.dot_general(
-            hidden, w_out_ref[...], (((1,), (1,)), ((), ())), preferred_element_type=f32
-        )
-        + bias_ref[...]
-    )
-    top = jnp.max(logits, axis=1, keepdims=True)
-    shifted = logits - top
-    powers = jnp.exp(shifted)
-    total = jnp.sum(powers, axis=1, keepdims=True)
-    log_total = jnp.log(total)
-    word = iota((rows * kept, vocab), 1)
-    is_label = word == emitted
-    blank_logp = shifted[:, 0:1] - log_total
-    label_logp = jnp.sum(jnp.where(is_label, shifted, 0.0), axis=1, keepdims=True) - log_total
-    cot_blank = jnp.concatenate([cols[:, 2 + k : 3 + k] for k in range(kept)], axis=0)
-    cot_label = jnp.concatenate([cols[:, 2 + kept + k : 3 + kept + k] for k in range(kept)], axis=0)
-    scale = (cot_blank + cot_label) / total
-    dlogit = (
-        jnp.where(word == 0, cot_blank, 0.0) + jnp.where(is_label, cot_label, 0.0) - powers * scale
-    ).astype(bf16)
-
-    grad_w = lax.dot_general(
-        hidden, dlogit, (((0,), (0,)), ((), ())), preferred_element_type=f32
+    word = iota((rows, vocab), 1)
+    hiddens, hiddens_t, dlogits, blank_logps, label_logps = [], [], [], [], []
+    for k in range(kept):
+        span = slice(k * rows, (k + 1) * rows)
+        hidden = jnp.tanh(enc_joint + dec_rows[span]).astype(bf16)
+        logits = jnp.dot(hidden, w_out_t[...], preferred_element_type=f32) + bias_ref[...]
+        hiddens.append(hidden)
+        hiddens_t.append(hidden.T)
+        shifted = logits - jnp.max(logits, axis=1, keepdims=True)
+        powers = jnp.exp(shifted)
+        total = jnp.sum(powers, axis=1, keepdims=True)
+        log_total = jnp.log(total)
+        is_label = word == emitted[span]
+        blank_logps.append(shifted[:, 0:1] - log_total)
+        label_logps.append(
+            jnp.sum(jnp.where(is_label, shifted, 0.0), axis=1, keepdims=True) - log_total
+        )
+        cot_blank = cols[:, 2 + k : 3 + k]
+        cot_label = cols[:, 2 + kept + k : 3 + kept + k]
+        scale = (cot_blank + cot_label) / total
+        dlogits.append(
+            (
+                jnp.where(word == 0, cot_blank, 0.0)
+                + jnp.where(is_label, cot_label, 0.0)
+                - powers * scale
+            ).astype(bf16)
+        )
+
+    grad_w = jnp.dot(
+        jnp.concatenate(hiddens_t, axis=1),
+        jnp.concatenate(dlogits, axis=0),
+        preferred_element_type=f32,
     ).astype(bf16)
     inner, core = lax.rem(me, 2), lax.rem(part, 2)
     outer_at, y = me // 2, part // 2
@@ -308,20 +321,26 @@
 
     if reduce_here:
         core_send[...] = grad_w.reshape(core_send.shape)
-        core_step = send_sum(0, core_send.at[:, :, :, 1 - core], core_recv, other_core)
-        core_step.start()
+        core_steps = [
+            send_sum(4 + outer + at, core_send.at[at, :, :, 1 - core], core_recv.at[at], other_core)
+            for at in range(outer)
+        ]
+        for step in core_steps:
+            step.start()
     else:
         grad_w_ref[...] = grad_w.astype(f32)
         stores[3].start()
 
-    back = jnp.dot(dlogit, w_out_ref[...], preferred_element_type=f32)
-    hidden_f = hidden.astype(f32)
-    dz = back * (1.0 - hidden_f * hidden_f)
-    enc_grad = dz[0:rows]
-    for k in range(1, kept):
-        enc_grad = enc_grad + dz[k * rows : (k + 1) * rows]
+    dzs = []
+    for k in range(kept):
+        back = jnp.dot(dlogits[k], w_out_ref[...], preferred_element_type=f32)
+        hidden_f = hiddens[k].astype(f32)
+        dzs.append(back * (1.0 - hidden_f * hidden_f))
+    enc_grad = dzs[0]
+    for dz in dzs[1:]:
+        enc_grad = enc_grad + dz
     owned_grad = lax.dot_general(
-        enc_grad.astype(bf16), w_enc_ref[...], (((1,), (1,)), ((), ())), preferred_element_type=f32
+        enc_grad.astype(bf16), w_enc_t[...], (((1,), (0,)), ((), ())), preferred_element_type=f32
     ).astype(bf16)
     outgoing[...] = (
         jnp.dot(place, owned_grad, preferred_element_type=f32)
@@ -335,22 +354,24 @@
     returned[me] = outgoing[me]
 
     if reduce_here:
-        core_step.wait()
-        core_sum[...] = add(core_send[:, :, :, core], core_recv[...])
         low, high = pl.ds(0, half), pl.ds(half, half)
         first_steps = (
-            send_sum(1, core_sum.at[low, :, 1 - y], first_recv.at[0], other_y),
-            send_sum(2, core_sum.at[high, 1 - inner], first_recv.at[1], other_x),
-        )
-        for step in first_steps:
-            step.start()
-
-    dec_grad = jnp.dot(scatter_hot, dz.astype(bf16), preferred_element_type=f32)
+            send_sum(0, core_sum.at[low, :, 1 - y], first_recv.at[0], other_y),
+            send_sum(1, core_sum.at[high, 1 - inner], first_recv.at[1], other_x),
+        )
+        for part_at, blocks in enumerate((low, high)):
+            for step in core_steps[part_at * half : (part_at + 1) * half]:
+                step.wait()
+            core_sum[blocks] = add(core_send[blocks, :, :, core], core_recv[blocks])
+            first_steps[part_at].start()
+
+    dz_rows = jnp.concatenate([dz.astype(bf16) for dz in dzs], axis=0)
+    dec_grad = jnp.dot(scatter_hot, dz_rows, preferred_element_type=f32)
     gp_send[...] = (
         lax.dot_general(
             dec_grad.astype(bf16),
-            w_dec_ref[...],
-            (((1,), (1,)), ((), ())),
+            w_dec_t[...],
+            (((1,), (0,)), ((), ())),
             preferred_element_type=f32,
         )
         .astype(bf16)
@@ -362,22 +383,18 @@
     each(shards, lambda step: send_gp(step).start())
 
     if reduce_here:
-        for step in first_steps:
-            step.wait()
-        first_sum[0] = add(core_sum[low, :, y], first_recv[0])
-        first_sum[1] = add(core_sum[high, inner], first_recv[1])
         second_steps = (
-            send_sum(3, first_sum.at[0, :, 1 - inner], second_recv.at[0], other_x),
-            send_sum(4, first_sum.at[1, :, 1 - y], second_recv.at[1], other_y),
-        )
-        for step in second_steps:
-            step.start()
+            send_sum(2, first_sum.at[0, :, 1 - inner], second_recv.at[0], other_x),
+            send_sum(3, first_sum.at[1, :, 1 - y], second_recv.at[1], other_y),
+        )
+        kept_blocks = (core_sum.at[low, :, y], core_sum.at[high, inner])
+        for part_at in range(2):
+            first_steps[part_at].wait()
+            first_sum[part_at] = add(kept_blocks[part_at][...], first_recv[part_at])
+            second_steps[part_at].start()
 
     logp_cols = jnp.concatenate(
-        [blank_logp[k * rows : (k + 1) * rows] for k in range(kept)]
-        + [label_logp[k * rows : (k + 1) * rows] for k in range(kept)]
-        + [jnp.zeros((rows, 8 - 2 * kept), f32)],
-        axis=1,
+        blank_logps + label_logps + [jnp.zeros((rows, 8 - 2 * kept), f32)], axis=1
     )
     logp_ref[...] = logp_cols.T[: 2 * kept]
     stores[0].start()
@@ -392,7 +409,7 @@
             peer = lax.rem(outer_at + step, outer)
             last_steps.append(
                 send_sum(
-                    4 + step, last_sum.at[peer], last_recv.at[step], {"dp": 2 * peer + inner}
+                    3 + step, last_sum.at[peer], last_recv.at[step], {"dp": 2 * peer + inner}
                 )
             )
         for step in last_steps:
@@ -522,10 +539,13 @@
             pltpu.VMEM((shards, lab_part, width), bf16),
             pltpu.VMEM((shards, lab_part, width), bf16),
             *fetched,
+            pltpu.VMEM(w_out.shape, bf16),
+            pltpu.VMEM(w_enc.shape[::-1], bf16),
+            pltpu.VMEM(w_dec.shape[::-1], bf16),
             *(pltpu.VMEM(output.shape, output.dtype) for output in outputs),
             pltpu.SemaphoreType.DMA((2, 2, owners)),
             pltpu.SemaphoreType.DMA((2, 2, shards)),
-            pltpu.SemaphoreType.DMA((2, 5 + outer)),
+            pltpu.SemaphoreType.DMA((2, 4 + 2 * outer)),
             pltpu.SemaphoreType.DMA((len(arrays),)),
             pltpu.SemaphoreType.DMA((len(outputs),)),
         ],

time: 31.6 us -> 31.6 us (level)
  no operation moved by 1% of the time
where the time goes in v4:
time: 31.6 us; the launch traced here: 31.4 us
  Pallas kernels  30.7 us (97%)
  between operations  0.64 us (2%)
    pallas_call x1, Pallas kernels, shards_fn(): pl.pallas_call(functools.partial(joint_kernel, (owners, shards, cap, rows...  29.1 us
    pallas_call x1, Pallas kernels, shards_fn(): pl.pallas_call(finish_kernel, out_shape=tuple((jax.ShapeDtypeStruct(array...  1.66 us

profile of v4, /device:TPU:0, one launch (start us, length us, event | category | flops | bytes accessed | tf_op | source)
XLA Modules:
  0.0 31.4 jit_solution(2063663478882610330)
XLA Ops:
  0.6 29.1 %shard_map.147 = (f32[6,128]{1,0:T(8,128)}, bf16[128,512]{1,0:T(8,128)(2,1)}, f32[32,512]{1,0:T(8,128)}, f32[16,500]{1,0:T(8,128)}) custom-call(bf16[128,512]{1,0:T(8,128)(2,1)} %enc_hbm.1, s32[8,128]{1,0:T(8,128)} %bitcast.8, bf16[32,512]{1,0:T(8,128)(2,1)} %pred_ref.1, s32[1,128]{1,0:T(1,128)} %label_hbm.1, s32[2]{0:T(128)} %off_hbm.1, s32[1,128]{1,0:T(1,128)} %bitcast.12, ...), custom_call_target="tpu_custom_call" | custom-call | tf_op jit(solution)/shard_map/pallas_call | solution.py:520
  29.7 1.7 %shard_map.148 = (f32[6,128]{1,0:T(8,128)}, bf16[128,512]{1,0:T(8,128)(2,1)}, f32[32,512]{1,0:T(8,128)}, f32[16,500]{1,0:T(8,128)}) custom-call(f32[6,128]{1,0:T(8,128)} %get-tuple-element.12.refs_0_, bf16[128,512]{1,0:T(8,128)(2,1)} %get-tuple-element.13.refs_1_, f32[32,512]{1,0:T(8,128)} %get-tuple-element.14.refs_2_, f32[16,500]{1,0:T(8,128)} %get-tuple-element.15.refs_3_), custom_call_target="tpu_custom_call" | custom-call | tf_op jit(solution)/shard_map/pallas_call | solution.py:560

commit v5 on v4

--- a/solution.py
+++ b/solution.py
@@ -41,14 +41,10 @@
     outgoing,
     returned,
     pred_all,
-    core_send,
-    core_recv,
-    core_sum,
-    first_recv,
-    first_sum,
-    second_recv,
-    last_sum,
-    last_recv,
+    piece_send,
+    piece_recv,
+    owner_sum,
+    owner_recv,
     gp_send,
     gp_recv,
     enc_ref,
@@ -71,7 +67,8 @@
     grad_w_ref,
     dp_sem,
     frame_sem,
-    sum_sem,
+    piece_sem,
+    owner_sem,
     load_sem,
     store_sem,
 ):
@@ -298,35 +295,36 @@
         jnp.concatenate(dlogits, axis=0),
         preferred_element_type=f32,
     ).astype(bf16)
-    inner, core = lax.rem(me, 2), lax.rem(part, 2)
-    outer_at, y = me // 2, part // 2
-    outer = owners // 2
-    half = outer // 2
-    other_core = {"frame": part + 1 - 2 * core}
-    other_y = {"frame": lax.rem(part + 2, shards)}
-    other_x = {"dp": me + 1 - 2 * inner}
-
-    def send_sum(slot, src, dst, device):
+    inner, outer_at, outer = lax.rem(me, 2), me // 2, owners // 2
+    ahead = sorted(range(outer), key=lambda step: (step == 0, abs(2 * step - outer)))
+
+    def piece_copy(near, step):
+        peer = lax.rem(part + step, shards)
         return pltpu.make_async_remote_copy(
-            src_ref=src,
-            dst_ref=dst,
-            send_sem=sum_sem.at[0, slot],
-            recv_sem=sum_sem.at[1, slot],
-            device_id=device,
+            src_ref=piece_send.at[lax.rem(outer_at + near, outer), :, peer],
+            dst_ref=piece_recv.at[near, step],
+            send_sem=piece_sem.at[0, near, step],
+            recv_sem=piece_sem.at[1, near, step],
+            device_id={"frame": peer},
             device_id_type=MESH,
         )
 
-    def add(one, two):
-        return (one.astype(f32) + two.astype(f32)).astype(bf16)
+    def owner_copy(near, side):
+        to_inner = lax.rem(inner + side, 2)
+        return pltpu.make_async_remote_copy(
+            src_ref=owner_sum.at[near, to_inner],
+            dst_ref=owner_recv.at[near, side],
+            send_sem=owner_sem.at[0, near, side],
+            recv_sem=owner_sem.at[1, near, side],
+            device_id={"dp": 2 * lax.rem(outer_at + near, outer) + to_inner},
+            device_id_type=MESH,
+        )
 
     if reduce_here:
-        core_send[...] = grad_w.reshape(core_send.shape)
-        core_steps = [
-            send_sum(4 + outer + at, core_send.at[at, :, :, 1 - core], core_recv.at[at], other_core)
-            for at in range(outer)
-        ]
-        for step in core_steps:
-            step.start()
+        piece_send[...] = grad_w.reshape(piece_send.shape)
+        for near in ahead:
+            for step in range(1, shards):
+                piece_copy(near, step).start()
     else:
         grad_w_ref[...] = grad_w.astype(f32)
         stores[3].start()
@@ -353,18 +351,6 @@
     each(owners, lambda step: send_back(step).start())
     returned[me] = outgoing[me]
 
-    if reduce_here:
-        low, high = pl.ds(0, half), pl.ds(half, half)
-        first_steps = (
-            send_sum(0, core_sum.at[low, :, 1 - y], first_recv.at[0], other_y),
-            send_sum(1, core_sum.at[high, 1 - inner], first_recv.at[1], other_x),
-        )
-        for part_at, blocks in enumerate((low, high)):
-            for step in core_steps[part_at * half : (part_at + 1) * half]:
-                step.wait()
-            core_sum[blocks] = add(core_send[blocks, :, :, core], core_recv[blocks])
-            first_steps[part_at].start()
-
     dz_rows = jnp.concatenate([dz.astype(bf16) for dz in dzs], axis=0)
     dec_grad = jnp.dot(scatter_hot, dz_rows, preferred_element_type=f32)
     gp_send[...] = (
@@ -383,37 +369,21 @@
     each(shards, lambda step: send_gp(step).start())
 
     if reduce_here:
-        second_steps = (
-            send_sum(2, first_sum.at[0, :, 1 - inner], second_recv.at[0], other_x),
-            send_sum(3, first_sum.at[1, :, 1 - y], second_recv.at[1], other_y),
-        )
-        kept_blocks = (core_sum.at[low, :, y], core_sum.at[high, inner])
-        for part_at in range(2):
-            first_steps[part_at].wait()
-            first_sum[part_at] = add(kept_blocks[part_at][...], first_recv[part_at])
-            second_steps[part_at].start()
+        for near in ahead:
+            for step in range(1, shards):
+                piece_copy(near, step).wait()
+            piece = piece_send[lax.rem(outer_at + near, outer), :, part].astype(f32)
+            for step in range(1, shards):
+                piece = piece + piece_recv[near, step].astype(f32)
+            owner_sum[near] = piece.astype(bf16)
+            for side in range(near == 0, 2):
+                owner_copy(near, side).start()
 
     logp_cols = jnp.concatenate(
         blank_logps + label_logps + [jnp.zeros((rows, 8 - 2 * kept), f32)], axis=1
     )
     logp_ref[...] = logp_cols.T[: 2 * kept]
     stores[0].start()
-
-    if reduce_here:
-        for step in second_steps:
-            step.wait()
-        last_sum[low] = add(first_sum[0, :, inner], second_recv[0])
-        last_sum[high] = add(first_sum[1, :, y], second_recv[1])
-        last_steps = []
-        for step in range(1, outer):
-            peer = lax.rem(outer_at + step, outer)
-            last_steps.append(
-                send_sum(
-                    3 + step, last_sum.at[peer], last_recv.at[step], {"dp": 2 * peer + inner}
-                )
-            )
-        for step in last_steps:
-            step.start()
 
     each(shards, lambda step: send_gp(step).wait())
     pred_sum = gp_send[part].astype(f32)
@@ -429,11 +399,11 @@
     stores[2].start()
 
     if reduce_here:
-        for step in last_steps:
-            step.wait()
-        whole_sum = last_sum[outer_at].astype(f32)
-        for step in range(1, outer):
-            whole_sum = whole_sum + last_recv[step].astype(f32)
+        whole_sum = owner_sum[0, inner].astype(f32)
+        for near in ahead:
+            for side in range(near == 0, 2):
+                owner_copy(near, side).wait()
+                whole_sum = whole_sum + owner_recv[near, side].astype(f32)
         grad_w_ref[...] = whole_sum
         stores[3].start()
     for store in stores:
@@ -484,11 +454,10 @@
     lab_part = pred_rows.shape[0]
     cap = max(TILE_ROWS, 2 * rows // owners)
     per_device = joint // (owners * shards)
-    reduce_here = per_device % TILE_ROWS == 0 and owners % 4 == 0 and shards == 4
+    reduce_here = per_device % TILE_ROWS == 0 and owners % 2 == 0
     grad_rows = per_device if reduce_here else joint
     slot_rows = per_device if reduce_here else TILE_ROWS
-    outer = owners // 2 if reduce_here else 2
-    half = outer // 2
+    outer = owners // 2 if reduce_here else 1
     bf16 = jnp.bfloat16
     hbm = pl.BlockSpec(memory_space=pltpu.HBM)
     exchange = pltpu.VMEM((owners, cap, width), bf16)
@@ -528,14 +497,10 @@
             exchange,
             exchange,
             pltpu.VMEM((shards, lab_part, width), bf16),
-            pltpu.VMEM((outer, 2, 2, 2, slot_rows, vocab), bf16),
-            pltpu.VMEM((outer, 2, 2, slot_rows, vocab), bf16),
-            pltpu.VMEM((outer, 2, 2, slot_rows, vocab), bf16),
-            pltpu.VMEM((2, half, 2, slot_rows, vocab), bf16),
-            pltpu.VMEM((2, half, 2, slot_rows, vocab), bf16),
-            pltpu.VMEM((2, half, slot_rows, vocab), bf16),
-            pltpu.VMEM((outer, slot_rows, vocab), bf16),
-            pltpu.VMEM((outer, slot_rows, vocab), bf16),
+            pltpu.VMEM((outer, 2, shards, slot_rows, vocab), bf16),
+            pltpu.VMEM((outer, shards, 2, slot_rows, vocab), bf16),
+            pltpu.VMEM((outer, 2, slot_rows, vocab), bf16),
+            pltpu.VMEM((outer, 2, slot_rows, vocab), bf16),
             pltpu.VMEM((shards, lab_part, width), bf16),
             pltpu.VMEM((shards, lab_part, width), bf16),
             *fetched,
@@ -545,7 +510,8 @@
             *(pltpu.VMEM(output.shape, output.dtype) for output in outputs),
             pltpu.SemaphoreType.DMA((2, 2, owners)),
             pltpu.SemaphoreType.DMA((2, 2, shards)),
-            pltpu.SemaphoreType.DMA((2, 4 + 2 * outer)),
+            pltpu.SemaphoreType.DMA((2, outer, shards)),
+            pltpu.SemaphoreType.DMA((2, outer, 2)),
             pltpu.SemaphoreType.DMA((len(arrays),)),
             pltpu.SemaphoreType.DMA((len(outputs),)),
         ],

time: 31.6 us -> 29.2 us (0.924)
  Pallas kernels: 30.7 us -> 28.4 us
    pallas_call x1, Pallas kernels: 29.1 us -> 26.7 us  [shards_fn(): pl.pallas_call(functools.partial(joint_kernel, (owners, shards, cap, rows...]
where the time goes in v5:
time: 29.2 us; the launch traced here: 29 us
  Pallas kernels  28.4 us (97%)
  between operations  0.64 us (2%)
    pallas_call x1, Pallas kernels, shards_fn(): pl.pallas_call(functools.partial(joint_kernel, (owners, shards, cap, rows...  26.7 us
    pallas_call x1, Pallas kernels, shards_fn(): pl.pallas_call(finish_kernel, out_shape=tuple((jax.ShapeDtypeStruct(array...  1.66 us

profile of v5, /device:TPU:0, one launch (start us, length us, event | category | flops | bytes accessed | tf_op | source)
XLA Modules:
  0.0 29.0 jit_solution(5288627182712030275)
XLA Ops:
  0.6 26.7 %shard_map.147 = (f32[6,128]{1,0:T(8,128)}, bf16[128,512]{1,0:T(8,128)(2,1)}, f32[32,512]{1,0:T(8,128)}, f32[16,500]{1,0:T(8,128)}) custom-call(bf16[128,512]{1,0:T(8,128)(2,1)} %enc_hbm.1, s32[8,128]{1,0:T(8,128)} %bitcast.8, bf16[32,512]{1,0:T(8,128)(2,1)} %pred_ref.1, s32[1,128]{1,0:T(1,128)} %label_hbm.1, s32[2]{0:T(128)} %off_hbm.1, s32[1,128]{1,0:T(1,128)} %bitcast.12, ...), custom_call_target="tpu_custom_call" | custom-call | tf_op jit(solution)/shard_map/pallas_call | solution.py:489
  27.4 1.7 %shard_map.148 = (f32[6,128]{1,0:T(8,128)}, bf16[128,512]{1,0:T(8,128)(2,1)}, f32[32,512]{1,0:T(8,128)}, f32[16,500]{1,0:T(8,128)}) custom-call(f32[6,128]{1,0:T(8,128)} %get-tuple-element.12.refs_0_, bf16[128,512]{1,0:T(8,128)(2,1)} %get-tuple-element.13.refs_1_, f32[32,512]{1,0:T(8,128)} %get-tuple-element.14.refs_2_, f32[16,500]{1,0:T(8,128)} %get-tuple-element.15.refs_3_), custom_call_target="tpu_custom_call" | custom-call | tf_op jit(solution)/shard_map/pallas_call | solution.py:526

commit v6 on v5

--- a/solution.py
+++ b/solution.py
@@ -44,6 +44,8 @@
     piece_send,
     piece_recv,
     owner_sum,
+    pair_recv,
+    pair_sum,
     owner_recv,
     gp_send,
     gp_recv,
@@ -309,16 +311,41 @@
             device_id_type=MESH,
         )
 
-    def owner_copy(near, side):
-        to_inner = lax.rem(inner + side, 2)
+    def pair_copy(near):
         return pltpu.make_async_remote_copy(
-            src_ref=owner_sum.at[near, to_inner],
-            dst_ref=owner_recv.at[near, side],
-            send_sem=owner_sem.at[0, near, side],
-            recv_sem=owner_sem.at[1, near, side],
-            device_id={"dp": 2 * lax.rem(outer_at + near, outer) + to_inner},
+            src_ref=owner_sum.at[near, 1 - inner],
+            dst_ref=pair_recv.at[near],
+            send_sem=owner_sem.at[0, near, 0],
+            recv_sem=owner_sem.at[1, near, 0],
+            device_id={"dp": me + 1 - 2 * inner},
             device_id_type=MESH,
         )
+
+    def owner_copy(near):
+        return pltpu.make_async_remote_copy(
+            src_ref=pair_sum.at[near],
+            dst_ref=owner_recv.at[near],
+            send_sem=owner_sem.at[0, near, 1],
+            recv_sem=owner_sem.at[1, near, 1],
+            device_id={"dp": 2 * lax.rem(outer_at + near, outer) + inner},
+            device_id_type=MESH,
+        )
+
+    def sum_piece(near):
+        for step in range(1, shards):
+            piece_copy(near, step).wait()
+        piece = piece_send[lax.rem(outer_at + near, outer), :, part].astype(f32)
+        for step in range(1, shards):
+            piece = piece + piece_recv[near, step].astype(f32)
+        owner_sum[near] = piece.astype(bf16)
+        pair_copy(near).start()
+
+    def sum_pair(near):
+        pair_copy(near).wait()
+        pair = owner_sum[near, inner].astype(f32) + pair_recv[near].astype(f32)
+        pair_sum[near] = pair.astype(bf16)
+        if near:
+            owner_copy(near).start()
 
     if reduce_here:
         piece_send[...] = grad_w.reshape(piece_send.shape)
@@ -351,6 +378,12 @@
     each(owners, lambda step: send_back(step).start())
     returned[me] = outgoing[me]
 
+    if reduce_here:
+        for at, near in enumerate(ahead[:2]):
+            sum_piece(near)
+            if at:
+                sum_pair(ahead[at - 1])
+
     dz_rows = jnp.concatenate([dz.astype(bf16) for dz in dzs], axis=0)
     dec_grad = jnp.dot(scatter_hot, dz_rows, preferred_element_type=f32)
     gp_send[...] = (
@@ -369,15 +402,10 @@
     each(shards, lambda step: send_gp(step).start())
 
     if reduce_here:
-        for near in ahead:
-            for step in range(1, shards):
-                piece_copy(near, step).wait()
-            piece = piece_send[lax.rem(outer_at + near, outer), :, part].astype(f32)
-            for step in range(1, shards):
-                piece = piece + piece_recv[near, step].astype(f32)
-            owner_sum[near] = piece.astype(bf16)
-            for side in range(near == 0, 2):
-                owner_copy(near, side).start()
+        for at, near in enumerate(ahead[2:], 2):
+            sum_piece(near)
+            sum_pair(ahead[at - 1])
+        sum_pair(ahead[-1])
 
     logp_cols = jnp.concatenate(
         blank_logps + label_logps + [jnp.zeros((rows, 8 - 2 * kept), f32)], axis=1
@@ -399,11 +427,10 @@
     stores[2].start()
 
     if reduce_here:
-        whole_sum = owner_sum[0, inner].astype(f32)
-        for near in ahead:
-            for side in range(near == 0, 2):
-                owner_copy(near, side).wait()
-                whole_sum = whole_sum + owner_recv[near, side].astype(f32)
+        whole_sum = pair_sum[0].astype(f32)
+        for near in ahead[:-1]:
+            owner_copy(near).wait()
+            whole_sum = whole_sum + owner_recv[near].astype(f32)
         grad_w_ref[...] = whole_sum
         stores[3].start()
     for store in stores:
@@ -500,7 +527,9 @@
             pltpu.VMEM((outer, 2, shards, slot_rows, vocab), bf16),
             pltpu.VMEM((outer, shards, 2, slot_rows, vocab), bf16),
             pltpu.VMEM((outer, 2, slot_rows, vocab), bf16),
-            pltpu.VMEM((outer, 2, slot_rows, vocab), bf16),
+            pltpu.VMEM((outer, slot_rows, vocab), bf16),
+            pltpu.VMEM((outer, slot_rows, vocab), bf16),
+            pltpu.VMEM((outer, slot_rows, vocab), bf16),
             pltpu.VMEM((shards, lab_part, width), bf16),
             pltpu.VMEM((shards, lab_part, width), bf16),
             *fetched,

time: 29.2 us -> 30.5 us (1.045)
  Pallas kernels: 28.4 us -> 29.7 us
    pallas_call x1, Pallas kernels: 26.7 us -> 28 us  [shards_fn(): pl.pallas_call(functools.partial(joint_kernel, (owners, shards, cap, rows...]
where the time goes in v6:
time: 30.5 us; the launch traced here: 30.3 us
  Pallas kernels  29.7 us (97%)
  between operations  0.64 us (2%)
    pallas_call x1, Pallas kernels, shards_fn(): pl.pallas_call(functools.partial(joint_kernel, (owners, shards, cap, rows...  28 us
    pallas_call x1, Pallas kernels, shards_fn(): pl.pallas_call(finish_kernel, out_shape=tuple((jax.ShapeDtypeStruct(array...  1.66 us

profile of v6, /device:TPU:0, one launch (start us, length us, event | category | flops | bytes accessed | tf_op | source)
XLA Modules:
  0.0 30.3 jit_solution(12103923468739243)
XLA Ops:
  0.6 28.0 %shard_map.147 = (f32[6,128]{1,0:T(8,128)}, bf16[128,512]{1,0:T(8,128)(2,1)}, f32[32,512]{1,0:T(8,128)}, f32[16,500]{1,0:T(8,128)}) custom-call(bf16[128,512]{1,0:T(8,128)(2,1)} %enc_hbm.1, s32[8,128]{1,0:T(8,128)} %bitcast.8, bf16[32,512]{1,0:T(8,128)(2,1)} %pred_ref.1, s32[1,128]{1,0:T(1,128)} %label_hbm.1, s32[2]{0:T(128)} %off_hbm.1, s32[1,128]{1,0:T(1,128)} %bitcast.12, ...), custom_call_target="tpu_custom_call" | custom-call | tf_op jit(solution)/shard_map/pallas_call | solution.py:516
  28.7 1.7 %shard_map.148 = (f32[6,128]{1,0:T(8,128)}, bf16[128,512]{1,0:T(8,128)(2,1)}, f32[32,512]{1,0:T(8,128)}, f32[16,500]{1,0:T(8,128)}) custom-call(f32[6,128]{1,0:T(8,128)} %get-tuple-element.12.refs_0_, bf16[128,512]{1,0:T(8,128)(2,1)} %get-tuple-element.13.refs_1_, f32[32,512]{1,0:T(8,128)} %get-tuple-element.14.refs_2_, f32[16,500]{1,0:T(8,128)} %get-tuple-element.15.refs_3_), custom_call_target="tpu_custom_call" | custom-call | tf_op jit(solution)/shard_map/pallas_call | solution.py:555

commit v7 on v5

--- a/solution.py
+++ b/solution.py
@@ -42,6 +42,8 @@
     returned,
     pred_all,
     piece_send,
+    core_recv,
+    core_sum,
     piece_recv,
     owner_sum,
     owner_recv,
@@ -298,14 +300,25 @@
     inner, outer_at, outer = lax.rem(me, 2), me // 2, owners // 2
     ahead = sorted(range(outer), key=lambda step: (step == 0, abs(2 * step - outer)))
 
-    def piece_copy(near, step):
-        peer = lax.rem(part + step, shards)
+    core, y = lax.rem(part, 2), part // 2
+
+    def core_copy(near):
         return pltpu.make_async_remote_copy(
-            src_ref=piece_send.at[lax.rem(outer_at + near, outer), :, peer],
-            dst_ref=piece_recv.at[near, step],
-            send_sem=piece_sem.at[0, near, step],
-            recv_sem=piece_sem.at[1, near, step],
-            device_id={"frame": peer},
+            src_ref=piece_send.at[lax.rem(outer_at + near, outer), :, :, 1 - core],
+            dst_ref=core_recv.at[near],
+            send_sem=piece_sem.at[0, near, 0],
+            recv_sem=piece_sem.at[1, near, 0],
+            device_id={"frame": part + 1 - 2 * core},
+            device_id_type=MESH,
+        )
+
+    def piece_copy(near):
+        return pltpu.make_async_remote_copy(
+            src_ref=core_sum.at[near, :, 1 - y],
+            dst_ref=piece_recv.at[near],
+            send_sem=piece_sem.at[0, near, 1],
+            recv_sem=piece_sem.at[1, near, 1],
+            device_id={"frame": lax.rem(part + 2, shards)},
             device_id_type=MESH,
         )
 
@@ -323,8 +336,7 @@
     if reduce_here:
         piece_send[...] = grad_w.reshape(piece_send.shape)
         for near in ahead:
-            for step in range(1, shards):
-                piece_copy(near, step).start()
+            core_copy(near).start()
     else:
         grad_w_ref[...] = grad_w.astype(f32)
         stores[3].start()
@@ -351,6 +363,13 @@
     each(owners, lambda step: send_back(step).start())
     returned[me] = outgoing[me]
 
+    if reduce_here:
+        for near in ahead:
+            core_copy(near).wait()
+            own = piece_send[lax.rem(outer_at + near, outer), :, :, core].astype(f32)
+            core_sum[near] = (own + core_recv[near].astype(f32)).astype(bf16)
+            piece_copy(near).start()
+
     dz_rows = jnp.concatenate([dz.astype(bf16) for dz in dzs], axis=0)
     dec_grad = jnp.dot(scatter_hot, dz_rows, preferred_element_type=f32)
     gp_send[...] = (
@@ -370,11 +389,8 @@
 
     if reduce_here:
         for near in ahead:
-            for step in range(1, shards):
-                piece_copy(near, step).wait()
-            piece = piece_send[lax.rem(outer_at + near, outer), :, part].astype(f32)
-            for step in range(1, shards):
-                piece = piece + piece_recv[near, step].astype(f32)
+            piece_copy(near).wait()
+            piece = core_sum[near, :, y].astype(f32) + piece_recv[near].astype(f32)
             owner_sum[near] = piece.astype(bf16)
             for side in range(near == 0, 2):
                 owner_copy(near, side).start()
@@ -454,7 +470,7 @@
     lab_part = pred_rows.shape[0]
     cap = max(TILE_ROWS, 2 * rows // owners)
     per_device = joint // (owners * shards)
-    reduce_here = per_device % TILE_ROWS == 0 and owners % 2 == 0
+    reduce_here = per_device % TILE_ROWS == 0 and owners % 2 == 0 and shards == 4
     grad_rows = per_device if reduce_here else joint
     slot_rows = per_device if reduce_here else TILE_ROWS
     outer = owners // 2 if reduce_here else 1
@@ -497,8 +513,10 @@
             exchange,
             exchange,
             pltpu.VMEM((shards, lab_part, width), bf16),
-            pltpu.VMEM((outer, 2, shards, slot_rows, vocab), bf16),
-            pltpu.VMEM((outer, shards, 2, slot_rows, vocab), bf16),
+            pltpu.VMEM((outer, 2, shards // 2, 2, slot_rows, vocab), bf16),
+            pltpu.VMEM((outer, 2, shards // 2, slot_rows, vocab), bf16),
+            pltpu.VMEM((outer, 2, shards // 2, slot_rows, vocab), bf16),
+            pltpu.VMEM((outer, 2, slot_rows, vocab), bf16),
             pltpu.VMEM((outer, 2, slot_rows, vocab), bf16),
             pltpu.VMEM((outer, 2, slot_rows, vocab), bf16),
             pltpu.VMEM((shards, lab_part, width), bf16),
@@ -510,7 +528,7 @@
             *(pltpu.VMEM(output.shape, output.dtype) for output in outputs),
             pltpu.SemaphoreType.DMA((2, 2, owners)),
             pltpu.SemaphoreType.DMA((2, 2, shards)),
-            pltpu.SemaphoreType.DMA((2, outer, shards)),
+            pltpu.SemaphoreType.DMA((2, outer, 2)),
             pltpu.SemaphoreType.DMA((2, outer, 2)),
             pltpu.SemaphoreType.DMA((len(arrays),)),
             pltpu.SemaphoreType.DMA((len(outputs),)),

time: 29.2 us -> 28.5 us (0.976)
  Pallas kernels: 28.4 us -> 27.7 us
    pallas_call x1, Pallas kernels: 26.7 us -> 26 us  [shards_fn(): pl.pallas_call(functools.partial(joint_kernel, (owners, shards, cap, rows...]
where the time goes in v7:
time: 28.5 us; the launch traced here: 28.3 us
  Pallas kernels  27.7 us (97%)
  between operations  0.64 us (2%)
    pallas_call x1, Pallas kernels, shards_fn(): pl.pallas_call(functools.partial(joint_kernel, (owners, shards, cap, rows...  26 us
    pallas_call x1, Pallas kernels, shards_fn(): pl.pallas_call(finish_kernel, out_shape=tuple((jax.ShapeDtypeStruct(array...  1.66 us

profile of v7, /device:TPU:0, one launch (start us, length us, event | category | flops | bytes accessed | tf_op | source)
XLA Modules:
  0.0 28.3 jit_solution(3757206225114968595)
XLA Ops:
  0.6 26.0 %shard_map.147 = (f32[6,128]{1,0:T(8,128)}, bf16[128,512]{1,0:T(8,128)(2,1)}, f32[32,512]{1,0:T(8,128)}, f32[16,500]{1,0:T(8,128)}) custom-call(bf16[128,512]{1,0:T(8,128)(2,1)} %enc_hbm.1, s32[8,128]{1,0:T(8,128)} %bitcast.8, bf16[32,512]{1,0:T(8,128)(2,1)} %pred_ref.1, s32[1,128]{1,0:T(1,128)} %label_hbm.1, s32[2]{0:T(128)} %off_hbm.1, s32[1,128]{1,0:T(1,128)} %bitcast.12, ...), custom_call_target="tpu_custom_call" | custom-call | tf_op jit(solution)/shard_map/pallas_call | solution.py:505
  26.6 1.7 %shard_map.148 = (f32[6,128]{1,0:T(8,128)}, bf16[128,512]{1,0:T(8,128)(2,1)}, f32[32,512]{1,0:T(8,128)}, f32[16,500]{1,0:T(8,128)}) custom-call(f32[6,128]{1,0:T(8,128)} %get-tuple-element.12.refs_0_, bf16[128,512]{1,0:T(8,128)(2,1)} %get-tuple-element.13.refs_1_, f32[32,512]{1,0:T(8,128)} %get-tuple-element.14.refs_2_, f32[16,500]{1,0:T(8,128)} %get-tuple-element.15.refs_3_), custom_call_target="tpu_custom_call" | custom-call | tf_op jit(solution)/shard_map/pallas_call | solution.py:544
